TPU v7x, 32 devices: a whole 2x2x4 slice. The times are simulated.
32 devices in a mesh: row: 8 (over z, y), col: 4 (over x, core).
Axes of the slice: x: 2, y: 2, z: 4, core: 2. Of those that a mesh axis runs over, the one named last changes fastest.
Arguments:
- weight: bfloat16 [16384, 32768], P('row', 'col'), may hold values from -600 to 600
- basis_prev: bfloat16 [32768, 512], P(('col', 'row')), may hold values from -6 to 6
Outputs:
- left_basis: bfloat16 [16384, 512], P(('row', 'col'))
- right_factor: bfloat16 [32768, 512], P(('col', 'row'))
All inputs are finite; a program needn't handle non-finite values.
Results may differ from a plain program's by a relative error of at most 0.0042.
Values may be sent and summed in bfloat16 or wider, within the bound.
A program may use at most 128 MiB of HBM per device.

v0:
```python
import jax
import jax.numpy as jnp
from jax import lax
from jax.sharding import PartitionSpec as P

D = 16384


def gram_of(sketch):
    return jnp.dot(
        sketch.T, sketch, precision=lax.Precision.HIGHEST, preferred_element_type=jnp.float32
    )


def orthonormal(sketch, gram):
    lower = jnp.linalg.cholesky(gram / jnp.float32(D))
    solved = lax.linalg.triangular_solve(
        lower, sketch, left_side=False, lower=True, transpose_a=True
    )
    return solved.astype(jnp.bfloat16)


def per_device(weight, basis_prev):
    block = weight
    partial_sketch = jnp.dot(
        block,
        lax.all_gather(basis_prev, "row", axis=0, tiled=True),
        preferred_element_type=jnp.float32,
    )
    sketch = lax.psum_scatter(partial_sketch, "col", scatter_dimension=0, tiled=True)
    gram = lax.psum(gram_of(sketch), ("row", "col"))
    own_basis = orthonormal(sketch, gram)
    full_basis = lax.all_gather(own_basis, "col", axis=0, tiled=True)
    block = weight
    factor = lax.psum_scatter(
        lax.dot_general(
            block, full_basis, (((0,), (0,)), ((), ())), preferred_element_type=jnp.float32
        ),
        "row",
        scatter_dimension=0,
        tiled=True,
    )
    right_factor = (factor * jnp.float32(D ** (-0.5))).astype(jnp.bfloat16)
    return (own_basis, right_factor)


def solution(mesh):
    return jax.shard_map(
        per_device,
        mesh=mesh,
        in_specs=(P("row", "col"), P(("col", "row"), None)),
        out_specs=(P(("row", "col"), None), P(("col", "row"), None)),
        check_vma=False,
    )
```

profile of v0, /device:TPU:0, one launch (start us, length us, event | category | flops | bytes accessed | tf_op | source)
XLA Modules:
  0.0 826.8 jit_solution(15919993888093335436)
XLA Ops:
  7.9 129.9 %all-gather.3.cloned.1.call-done = bf16[8192,512]{1,0:T(8,128)(2,1)} async-done(((bf16[1024,512]{1,0:T(8,128)(2,1)}), bf16[8192,512]{1,0:T(8,128)(2,1)}) %all-gather.3.cloned.1.call-update) | async-done | bytes 8388624 | tf_op jit(solution)/shard_map/all_gather | solution.py:27
  137.8 24.7 %fusion.33 = f32[2048,512]{1,0:T(8,128)} fusion(bf16[2048,8192]{1,0:T(8,128)(2,1)} %param.2, bf16[8192,512]{1,0:T(8,128)(2,1)} %all-gather.3.cloned.1.call-done), kind=kOutput, calls=%fused_computation.73 | convolution fusion | flops 17179869184 | bytes 46137344 | tf_op jit(solution)/shard_map/dot_general | solution.py:25
  162.6 42.8 %reduce-scatter.3.cloned.1.call-done = f32[512,512]{1,0:T(8,128)} async-done(((f32[2048,512]{1,0:T(8,128)}), f32[512,512]{1,0:T(8,128)}) %reduce-scatter.3.cloned.1.call-update) | async-done | bytes 1048592 | tf_op jit(solution)/shard_map/reduce_scatter | solution.py:30
  205.4 4.4 fusion.34
  210.4 131.5 %all-reduce.3.cloned.1.call-done = f32[512,512]{0,1:T(8,128)} async-done(((f32[512,512]{0,1:T(8,128)}), f32[512,512]{0,1:T(8,128)}) %all-reduce.3.cloned.1.call-update) | async-done | bytes 1048592 | tf_op jit(solution)/shard_map/psum | solution.py:31
  341.8 1.3 broadcast_multiply_fusion
  343.5 1.5 fusion
  345.0 11.7 %cholesky.104 = f32[128,128]{1,0:T(8,128)S(1)} custom-call(f32[128,128]{1,0:T(8,128)S(1)} %cholesky.266), custom_call_target="Cholesky" | custom-call | tf_op jit(solution)/shard_map/jit(cholesky)/cholesky | solution.py:16
  356.7 9.8 %custom-call.30 = f32[1,128,128]{1,2,0:T(8,128)S(1)} custom-call(f32[1,128,128]{2,1,0:T(8,128)S(1)} %get-tuple-element.31), custom_call_target="InvertDiagBlocksLowerTriangular" | custom-call | tf_op jit(solution)/shard_map/jit(cholesky)/cholesky | solution.py:16
  367.3 11.7 %cholesky.217 = f32[128,128]{1,0:T(8,128)S(1)} custom-call(f32[128,128]{1,0:T(8,128)S(1)} %cholesky.270), custom_call_target="Cholesky" | custom-call | tf_op jit(solution)/shard_map/jit(cholesky)/cholesky | solution.py:16
  379.1 9.9 %custom-call.31 = f32[1,128,128]{1,2,0:T(8,128)S(1)} custom-call(f32[1,128,128]{2,1,0:T(8,128)S(1)} %get-tuple-element.28), custom_call_target="InvertDiagBlocksLowerTriangular" | custom-call | tf_op jit(solution)/shard_map/jit(cholesky)/cholesky | solution.py:16
  389.7 11.7 %cholesky.238 = f32[128,128]{1,0:T(8,128)S(1)} custom-call(f32[128,128]{1,0:T(8,128)S(1)} %cholesky.275), custom_call_target="Cholesky" | custom-call | tf_op jit(solution)/shard_map/jit(cholesky)/cholesky | solution.py:16
  401.4 0.7 compare_reduce_fusion.1
  402.2 9.8 %custom-call.32 = f32[1,128,128]{1,2,0:T(8,128)S(1)} custom-call(f32[1,128,128]{2,1,0:T(8,128)S(1)} %get-tuple-element.25), custom_call_target="InvertDiagBlocksLowerTriangular" | custom-call | tf_op jit(solution)/shard_map/jit(cholesky)/cholesky | solution.py:16
  412.6 11.7 %cholesky.255 = f32[128,128]{1,0:T(8,128)S(1)} custom-call(f32[128,128]{1,0:T(8,128)S(1)} %convolution_subtract_fusion.5), custom_call_target="Cholesky" | custom-call | tf_op jit(solution)/shard_map/jit(cholesky)/cholesky | solution.py:16
  425.0 0.9 compare_reduce_fusion.2
  428.5 10.9 %while.1 = (s32[]{:T(128)}, f32[512,512]{1,0:T(8,128)S(1)}, s32[4,2]{0,1:T(2,128)S(1)}, f32[4,128,128]{2,1,0:T(8,128)}, s32[]{:T(128)}) while((s32[]{:T(128)}, f32[512,512]{1,0:T(8,128)S(1)}, s32[4,2]{0,1:T(2,128)S(1)}, f32[4,128,128]{2,1,0:T(8,128)}, s32[]{:T(128)}) %tuple.35), condition=%wide.while_cond, body=%wide.while_body.sunk | while | flops 2 | bytes 132205 | solution.py:17
  429.2 2.1 bitcast_dynamic-update-slice_fusion.2
  431.9 2.1 bitcast_dynamic-update-slice_fusion.2
  434.6 2.1 bitcast_dynamic-update-slice_fusion.2
  437.4 2.1 bitcast_dynamic-update-slice_fusion.2
  439.4 40.1 %custom-call.33 = f32[4,128,128]{1,2,0:T(8,128)S(1)} custom-call(f32[4,128,128]{2,1,0:T(8,128)} %get-tuple-element.9), custom_call_target="InvertDiagBlocksLowerTriangular" | custom-call | tf_op jit(solution)/shard_map/triangular_solve | solution.py:17
  481.0 1.0 convolution_subtract_fusion
  482.4 1.5 convolution_subtract_fusion.2
  484.3 0.8 pad_maximum_fusion
  485.5 21.4 %all-gather.5.cloned.1.call-done = bf16[2048,512]{0,1:T(8,128)(2,1)} async-done(((bf16[512,512]{0,1:T(8,128)(2,1)}), bf16[2048,512]{0,1:T(8,128)(2,1)}) %all-gather.5.cloned.1.call-update) | async-done | bytes 2097168 | tf_op jit(solution)/shard_map/all_gather | solution.py:33
  506.9 27.2 %convolution_bitcast_fusion = f32[8192,512]{0,1:T(8,128)} fusion(bf16[2048,512]{0,1:T(8,128)(2,1)} %all-gather.5.cloned.1.call-done, bf16[2048,8192]{1,0:T(8,128)(2,1)} %param.2), kind=kOutput, calls=%fused_computation.2 | convolution fusion | flops 17179869184 | bytes 52428800 | tf_op jit(solution)/shard_map/dot_general | solution.py:36
  534.1 1.0 copy-done.1
  535.1 1.0 copy.6
  536.1 280.7 %reduce-scatter.5.cloned.1.call-done = f32[1024,512]{0,1:T(8,128)} async-done(((f32[8192,512]{0,1:T(8,128)}), f32[1024,512]{0,1:T(8,128)}) %reduce-scatter.5.cloned.1.call-update) | async-done | bytes 2097168 | tf_op jit(solution)/shard_map/reduce_scatter | solution.py:35
  816.9 1.8 multiply_convert_fusion
  818.7 1.3 copy.7
  (46 shorter events, 9.9 us)
Async XLA Ops:
  7.2 130.6 %all-gather.3.cloned.1.call-start = ((), (), s32[]{:S(2)}) async-start(), calls=%async_computation.2 | async-start | bytes 9437184 | tf_op jit(solution)/shard_map/all_gather | solution.py:27
  7.9 197.5 %reduce-scatter.3.cloned.1.call-start = ((), (), s32[]{:S(2)}) async-start(), calls=%async_computation.3 | async-start | bytes 5242880 | tf_op jit(solution)/shard_map/reduce_scatter | solution.py:30
  162.5 179.3 %all-reduce.3.cloned.1.call-start = ((), (), s32[]{:S(2)}) async-start(), calls=%async_computation.4 | async-start | bytes 2097152 | tf_op jit(solution)/shard_map/psum | solution.py:31
  209.7 269.8 %copy-start = (f32[512,512]{1,0:T(8,128)S(1)}, f32[512,512]{1,0:T(8,128)}, u32[]{:S(2)}) copy-start(f32[512,512]{1,0:T(8,128)} %reduce-scatter.3.cloned.1.call-done) | copy-start | bytes 3145732
  209.8 297.1 %all-gather.5.cloned.1.call-start = ((), (), s32[]{:S(2)}) async-start(), calls=%async_computation.5 | async-start | bytes 2621440 | tf_op jit(solution)/shard_map/all_gather | solution.py:33
  485.2 331.7 %reduce-scatter.5.cloned.1.call-start = ((), (), s32[]{:S(2)}) async-start(), calls=%async_computation.6 | async-start | bytes 18874368 | tf_op jit(solution)/shard_map/reduce_scatter | solution.py:35
  534.1 1.0 copy-start.1
Sparse Core Ops, SparseCore 0:
  10.1 127.6 all-gather.2
  162.6 42.6 reduce-scatter.2
  212.0 129.8 all-reduce.2
  485.3 21.5 all-gather.4
  534.2 282.5 reduce-scatter.4
where the time goes:
time: 831 us; the launch traced here: 827 us
  waiting for transfers between devices  607 us (73%)
  other arithmetic  124 us (15%)
  matrix products  62.9 us (8%)
  between operations  16.8 us (2%)
  local copies, waits for them, and re-layouts  14.7 us (2%)
    reduce_scatter x1, waiting for transfers between devices, per_device(): lax.psum_scatter(lax.dot_general(block, full_basis, (((0,), (0,)), ((), (...  281 us
    psum x1, waiting for transfers between devices, per_device(): gram = lax.psum(gram_of(sketch), ('row', 'col'))  131 us
    all_gather x1, waiting for transfers between devices, per_device(): lax.all_gather(basis_prev, 'row', axis=0, tiled=True)  130 us
    another operation x14, other arithmetic, orthonormal(): lower = jnp.linalg.cholesky(gram / jnp.float32(D))  78.8 us
    reduce_scatter x1, waiting for transfers between devices, per_device(): lax.psum_scatter(partial_sketch, 'col', scatter_dimension=0, tiled=True)  42.8 us
    another operation x4, other arithmetic, orthonormal(): lax.linalg.triangular_solve(lower, sketch, left_side=False, lower=True, t...  41.1 us
    dot_general x1, matrix products, per_device(): lax.dot_general(block, full_basis, (((0,), (0,)), ((), ())), preferred_el...  27.2 us
    dot_general x1, matrix products, per_device(): jnp.dot(block, lax.all_gather(basis_prev, 'row', axis=0, tiled=True), pre...  24.7 us
  transfers between devices with their start and end apart: 5, of which 5 were waited for; matrix products, arithmetic and copies ran while one was open for 0% of the time, Pallas kernels for 0%

commit v1 on v0

v1 whole, which is shorter than its diff:
```python
import jax
import jax.numpy as jnp
from jax import lax
from jax.sharding import PartitionSpec as P

F32 = jnp.float32
BF16 = jnp.bfloat16
HIGH = lax.Precision.HIGHEST


def dot(a, b, dims, precision=None):
    return lax.dot_general(a, b, ((dims[0], dims[1]), ((), ())), precision=precision,
                           preferred_element_type=F32)


def pair_of(n):
    return [(i, i ^ 1) for i in range(n)]


def ring_of(n):
    return [(i, (i + 2) % n) for i in range(n)]


def rows_of(x, start, count):
    return lax.dynamic_slice_in_dim(x, start, count, 0)


def all_sum(gram, sizes):
    steps = []
    held = gram
    for axis, n in sizes:
        bit = 1
        while bit < n:
            half = held.shape[0] // 2
            mine = (lax.axis_index(axis) // bit) % 2
            pairs = [(i, i ^ bit) for i in range(n)]
            got = lax.ppermute(rows_of(held, (1 - mine) * half, half), axis, pairs)
            held = rows_of(held, mine * half, half) + got
            steps.append((axis, pairs, mine))
            bit *= 2
    for axis, pairs, mine in reversed(steps):
        got = lax.ppermute(held, axis, pairs)
        low = jnp.where(mine == 0, held, got)
        high = jnp.where(mine == 0, got, held)
        held = jnp.concatenate([low, high], 0)
    return held


def inverse_factor(gram):
    n = gram.shape[0]
    b = 128
    eye = jnp.eye(b, dtype=F32)
    rest = gram
    rows = []
    panels = []
    count = n // b
    for i in range(count):
        head = rest[:b, :b]
        low = lax.linalg.cholesky(head, symmetrize_input=False)
        inv = lax.linalg.triangular_solve(low, eye, left_side=True, lower=True)
        if i + 1 < count:
            panel = dot(rest[b:, :b], inv, ((1,), (1,)), HIGH)
            rest = rest[b:, b:] - dot(panel, panel, ((1,), (1,)), HIGH)
            panels.append(panel)
        left = jnp.zeros((b, i * b), F32)
        if i:
            own = jnp.concatenate([panels[j][(i - 1 - j) * b:(i - j) * b] for j in range(i)], 1)
            left = -dot(inv, dot(own, jnp.concatenate(rows, 0)[:, :i * b], ((1,), (0,)), HIGH),
                        ((1,), (0,)), HIGH)
        rows.append(jnp.concatenate([left, inv, jnp.zeros((b, n - (i + 1) * b), F32)], 1))
    return jnp.concatenate(rows, 0)


def per_device(n_row, n_col, d, weight, basis_prev):
    depth, rank = basis_prev.shape
    me = lax.axis_index("row")
    group, side = me // 2, me % 2
    ring = n_row // 2

    held = basis_prev
    partial = None
    for step in range(ring):
        other = lax.ppermute(held, "row", pair_of(n_row))
        later = lax.ppermute(held, "row", ring_of(n_row)) if step + 1 < ring else None
        owner = (group - step + ring) % ring
        both = jnp.concatenate([jnp.where(side == 0, held, other), jnp.where(side == 0, other, held)], 0)
        cut = lax.dynamic_slice_in_dim(weight, owner * 2 * depth, 2 * depth, 1)
        term = dot(cut, both, ((1,), (0,)))
        partial = term if partial is None else partial + term
        held = later

    rows = weight.shape[0] // n_col
    col = lax.axis_index("col")
    cgroup, cside = col // 2, col % 2
    cring = n_col // 2
    parts = partial.reshape(cring, 2, rows, rank)
    away = lax.dynamic_index_in_dim(parts, 1 - cside, 1, keepdims=False)
    near = lax.dynamic_index_in_dim(parts, cside, 1, keepdims=False)
    near = near + lax.ppermute(away, "col", pair_of(n_col))
    sketch = None
    for step in range(cring):
        at = (cgroup - 1 - step + 2 * cring) % cring
        own = lax.dynamic_index_in_dim(near, at, 0, keepdims=False)
        sketch = own if sketch is None else own + sketch.astype(F32)
        if step + 1 < cring:
            sketch = lax.ppermute(sketch.astype(BF16), "col", ring_of(n_col))

    full = jnp.zeros((cring, 2, rows, rank), BF16)
    held = sketch.astype(BF16)
    for step in range(cring):
        other = lax.ppermute(held, "col", pair_of(n_col))
        later = lax.ppermute(held, "col", ring_of(n_col)) if step + 1 < cring else None
        two = jnp.stack([jnp.where(cside == 0, held, other), jnp.where(cside == 0, other, held)])
        full = lax.dynamic_update_slice(full, two[None], ((cgroup - step + cring) % cring, 0, 0, 0))
        held = later
    full = full.reshape(n_col * rows, rank)

    gram = dot(sketch, sketch, ((0,), (0,)), HIGH)
    gram = all_sum(gram, (("col", n_col), ("row", n_row)))
    inverse = inverse_factor(gram / F32(d))

    factor = None
    for step in range(ring):
        at = (group - 1 - step + 2 * ring) % ring
        cut = lax.dynamic_slice_in_dim(weight, at * 2 * depth, 2 * depth, 1)
        term = dot(cut, full, ((0,), (0,)))
        got = lax.ppermute(rows_of(term, (1 - side) * depth, depth).astype(BF16), "row", pair_of(n_row))
        term = rows_of(term, side * depth, depth) + got.astype(F32)
        factor = term if factor is None else term + factor.astype(F32)
        if step + 1 < ring:
            factor = lax.ppermute(factor.astype(BF16), "row", ring_of(n_row))

    left_basis = dot(sketch, inverse, ((1,), (1,)), HIGH).astype(BF16)
    right = dot(factor, inverse, ((1,), (1,)), HIGH)
    return left_basis, (right * F32(d ** (-0.5))).astype(BF16)


def solution(mesh):
    n_row, n_col = mesh.shape["row"], mesh.shape["col"]

    def run(weight, basis_prev):
        def body(w, b):
            return per_device(n_row, n_col, weight.shape[0], w, b)

        return jax.shard_map(
            body,
            mesh=mesh,
            in_specs=(P("row", "col"), P(("col", "row"), None)),
            out_specs=(P(("row", "col"), None), P(("col", "row"), None)),
            check_vma=False,
        )(weight, basis_prev)

    return run
```

time: 831 us -> 401 us (0.48)
  waiting for transfers between devices: 607 us -> 153 us
  matrix products: 62.9 us -> 89.4 us
  starting transfers between devices: 0.98 us -> 21.4 us
  between operations: 16.8 us -> 1.82 us
    reduce_scatter x2 -> x0, waiting for transfers between devices: 323 us -> none  [the longest x1 281 us: per_device(): lax.psum_scatter(lax.dot_general(block, full_basis, (((0,), (0,)), ((), (...]
    ppermute x0 -> x29, waiting for transfers between devices: none -> 153 us  [the longest x3 43.6 us: per_device(): lax.ppermute(held, 'row', ring_of(n_row))]
    all_gather x2 -> x0, waiting for transfers between devices: 151 us -> none  [the longest x1 130 us: per_device(): lax.all_gather(basis_prev, 'row', axis=0, tiled=True)]
    psum x1 -> x0, waiting for transfers between devices: 131 us -> none  [per_device(): gram = lax.psum(gram_of(sketch), ('row', 'col'))]
    dot_general x3 -> x23, matrix products: 56.3 us -> 87.5 us  [dot(): lax.dot_general(a, b, ((dims[0], dims[1]), ((), ())), precision=precision...]
    another operation x18 -> x22, other arithmetic: 120 us -> 97.2 us  [the longest x12 51.7 us: inverse_factor(): low = lax.linalg.cholesky(head, symmetrize_input=False)]
    ppermute x0 -> x29, starting transfers between devices: none -> 21.4 us  [the longest x4 4.82 us: per_device(): other = lax.ppermute(held, 'row', pair_of(n_row))]
    another operation x17 -> x4, local copies, waits for them, and re-layouts: 11.1 us -> 0.27 us  [the longest x3 0.27 us: inverse_factor(): inv = lax.linalg.triangular_solve(low, eye, left_side=True, lower=True)]
  transfers between devices with their start and end apart: 5 -> 29, of which waited for: 5 -> 16; matrix products, arithmetic and copies ran while one was open for 0% -> 47% of each run, Pallas kernels for 0% -> 0%
where the time goes in v1:
time: 401 us; the launch traced here: 393 us
  waiting for transfers between devices  153 us (38%)
  other arithmetic  116 us (29%)
  matrix products  89.4 us (22%)
  starting transfers between devices  21.4 us (5%)
  local copies, waits for them, and re-layouts  11.3 us (3%)
    dot_general x23, matrix products, dot(): lax.dot_general(a, b, ((dims[0], dims[1]), ((), ())), precision=precision...  87.5 us
    another operation x12, other arithmetic, inverse_factor(): low = lax.linalg.cholesky(head, symmetrize_input=False)  51.7 us
    another operation x8, other arithmetic, inverse_factor(): inv = lax.linalg.triangular_solve(low, eye, left_side=True, lower=True)  44.3 us
    ppermute x3, waiting for transfers between devices, per_device(): lax.ppermute(held, 'row', ring_of(n_row))  43.6 us
    ppermute x3, waiting for transfers between devices, per_device(): factor = lax.ppermute(factor.astype(BF16), 'row', ring_of(n_row))  34.6 us
    ppermute x4, waiting for transfers between devices, per_device(): other = lax.ppermute(held, 'row', pair_of(n_row))  26.4 us
    ppermute x5, waiting for transfers between devices, all_sum(): got = lax.ppermute(rows_of(held, (1 - mine) * half, half), axis, pairs)  15 us
    ppermute x1, waiting for transfers between devices, per_device(): sketch = lax.ppermute(sketch.astype(BF16), 'col', ring_of(n_col))  13.3 us
  transfers between devices with their start and end apart: 29, of which 16 were waited for; matrix products, arithmetic and copies ran while one was open for 47% of the time, Pallas kernels for 0%

profile of v1, /device:TPU:0, one launch (start us, length us, event | category | flops | bytes accessed | tf_op | source)
XLA Modules:
  0.0 393.4 jit_solution(3758602337273756438)
XLA Ops:
  5.2 23.9 %collective-permute-done.1 = bf16[1024,512]{1,0:T(8,128)(2,1)S(1)} collective-permute-done((bf16[1024,512]{1,0:T(8,128)(2,1)}, bf16[1024,512]{1,0:T(8,128)(2,1)S(1)}, u32[]{:S(2)}, u32[]{:S(2)}) %collective-permute-start.1) | collective-permute-done | bytes 1048608 | tf_op jit(solution)/shard_map/ppermute | solution.py:84
  32.0 6.9 %fusion.14 = f32[2048,512]{1,0:T(8,128)S(1)} fusion(bf16[2048,8192]{1,0:T(8,128)(2,1)} %param.5, s32[]{:T(128)S(6)} %select_n.297, bf16[1024,512]{1,0:T(8,128)(2,1)S(1)} %get-tuple-element.9, bf16[1024,512]{1,0:T(8,128)(2,1)S(1)} %get-tuple-element.8), kind=kOutput, calls=%fused_computation.14 | convolution fusion | flops 4299161600 | bytes 14680068 | tf_op jit(solution)/shard_map/dot_general | solution.py:12
  38.9 17.4 %collective-permute-done.3 = bf16[1024,512]{1,0:T(8,128)(2,1)S(1)} collective-permute-done((bf16[1024,512]{1,0:T(8,128)(2,1)S(1)}, bf16[1024,512]{1,0:T(8,128)(2,1)S(1)}, u32[]{:S(2)}, u32[]{:S(2)}) %collective-permute-start.3) | collective-permute-done | bytes 1048608 | tf_op jit(solution)/shard_map/ppermute | solution.py:84
  57.3 6.9 %fusion.10 = f32[2048,512]{1,0:T(8,128)S(1)} fusion(bf16[2048,8192]{1,0:T(8,128)(2,1)} %param.5, s32[]{:T(128)S(6)} %select_n.303, bf16[1024,512]{1,0:T(8,128)(2,1)S(1)} %get-tuple-element.7, bf16[1024,512]{1,0:T(8,128)(2,1)S(1)} %get-tuple-element.6), kind=kOutput, calls=%fused_computation.10 | convolution fusion | flops 4299161600 | bytes 14680068 | tf_op jit(solution)/shard_map/dot_general | solution.py:12
  64.2 15.0 %collective-permute-done.4 = bf16[1024,512]{1,0:T(8,128)(2,1)S(1)} collective-permute-done((bf16[1024,512]{1,0:T(8,128)(2,1)S(1)}, bf16[1024,512]{1,0:T(8,128)(2,1)S(1)}, u32[]{:S(2)}, u32[]{:S(2)}) %collective-permute-start.4) | collective-permute-done | bytes 1048608 | tf_op jit(solution)/shard_map/ppermute | solution.py:83
  82.7 9.5 %fusion.8 = f32[2048,512]{1,0:T(8,128)} fusion(bf16[2048,8192]{1,0:T(8,128)(2,1)} %param.5, s32[]{:T(128)S(6)} %select_n.307, bf16[1024,512]{1,0:T(8,128)(2,1)S(1)} %get-tuple-element.11, bf16[1024,512]{1,0:T(8,128)(2,1)S(1)} %get-tuple-element.10), kind=kOutput, calls=%fused_computation.8 | convolution fusion | flops 4299161600 | bytes 14680068 | tf_op jit(solution)/shard_map/dot_general | solution.py:12
  92.2 11.4 %collective-permute-done.6 = bf16[1024,512]{1,0:T(8,128)(2,1)S(1)} collective-permute-done((bf16[1024,512]{1,0:T(8,128)(2,1)S(1)}, bf16[1024,512]{1,0:T(8,128)(2,1)S(1)}, u32[]{:S(2)}, u32[]{:S(2)}) %collective-permute-start.6) | collective-permute-done | bytes 1048608 | tf_op jit(solution)/shard_map/ppermute | solution.py:83
  103.9 12.6 %add_add_fusion = f32[2048,512]{1,0:T(8,128)S(1)} fusion(f32[2048,512]{1,0:T(8,128)} %fusion.8, f32[2048,512]{1,0:T(8,128)S(1)} %fusion.14, f32[2048,512]{1,0:T(8,128)S(1)} %fusion.10, bf16[2048,8192]{1,0:T(8,128)(2,1)} %param.5, s32[]{:T(128)S(6)} %select_n.311, bf16[1024,512]{1,0:T(8,128)(2,1)S(1)} %get-tuple-element.5, ...), kind=kOutput, calls=%fused_computation.16 | convolution fusion | flops 4302307328 | bytes 27262980 | tf_op jit(solution)/shard_map/dot_general | solution.py:12
  118.8 4.2 %collective-permute-done.7 = f32[2,512,512]{2,1,0:T(8,128)} collective-permute-done((f32[2,512,512]{2,1,0:T(8,128)S(1)}, f32[2,512,512]{2,1,0:T(8,128)}, u32[]{:S(2)}, u32[]{:S(2)}) %collective-permute-start.7) | collective-permute-done | bytes 2097184 | tf_op jit(solution)/shard_map/ppermute | solution.py:99
  126.6 13.3 %collective-permute-done.8 = bf16[512,512]{1,0:T(8,128)(2,1)} collective-permute-done((bf16[512,512]{1,0:T(8,128)(2,1)S(1)}, bf16[512,512]{1,0:T(8,128)(2,1)}, u32[]{:S(2)}, u32[]{:S(2)}) %collective-permute-start.8) | collective-permute-done | bytes 524320 | tf_op jit(solution)/shard_map/ppermute | solution.py:106
  148.9 7.6 %collective-permute-done.10 = f32[128,512]{1,0:T(8,128)S(1)} collective-permute-done((f32[128,512]{1,0:T(8,128)S(1)}, f32[128,512]{1,0:T(8,128)S(1)}, u32[]{:S(2)}, u32[]{:S(2)}) %collective-permute-start.10) | collective-permute-done | bytes 262176 | tf_op jit(solution)/shard_map/ppermute | solution.py:37
  163.9 8.6 %collective-permute-done.20 = bf16[512,512]{1,0:T(8,128)(2,1)S(1)} collective-permute-done((bf16[512,512]{1,0:T(8,128)(2,1)S(1)}, bf16[512,512]{1,0:T(8,128)(2,1)S(1)}, u32[]{:S(2)}, u32[]{:S(2)}) %collective-permute-start.20) | collective-permute-done | bytes 524320 | tf_op jit(solution)/shard_map/ppermute | solution.py:112
  173.8 3.7 collective-permute-done.13
  177.9 4.4 %collective-permute-done.14 = f32[16,512]{1,0:T(8,128)S(1)} collective-permute-done((f32[16,512]{1,0:T(8,128)S(1)}, f32[16,512]{1,0:T(8,128)S(1)}, u32[]{:S(2)}, u32[]{:S(2)}) %collective-permute-start.14) | collective-permute-done | bytes 32800 | tf_op jit(solution)/shard_map/ppermute | solution.py:42
  182.5 6.9 %fusion.12 = f32[2048,512]{1,0:T(8,128)S(1)} fusion(bf16[2048,512]{1,0:T(8,128)(2,1)S(1)} %bitcast.72, bf16[2048,8192]{1,0:T(8,128)(2,1)} %param.5, s32[]{:T(128)S(6)} %select_n.297), kind=kOutput, calls=%fused_computation.12 | convolution fusion | flops 4294967296 | bytes 14680068 | tf_op jit(solution)/shard_map/dot_general | solution.py:12
  189.5 8.5 %fusion = f32[2048,512]{1,0:T(8,128)S(1)} fusion(bf16[2048,512]{1,0:T(8,128)(2,1)S(1)} %bitcast.73, bf16[2048,8192]{1,0:T(8,128)(2,1)} %param.5, s32[]{:T(128)S(6)} %select_n.369), kind=kOutput, calls=%fused_computation | convolution fusion | flops 4294967296 | bytes 14680068 | tf_op jit(solution)/shard_map/dot_general | solution.py:12
  206.0 6.9 %fusion.2 = f32[2048,512]{1,0:T(8,128)S(1)} fusion(bf16[2048,512]{1,0:T(8,128)(2,1)S(1)} %bitcast.74, bf16[2048,8192]{1,0:T(8,128)(2,1)} %param.5, s32[]{:T(128)S(6)} %select_n.367), kind=kOutput, calls=%fused_computation.2 | convolution fusion | flops 4294967296 | bytes 14680068 | tf_op jit(solution)/shard_map/dot_general | solution.py:12
  215.0 7.2 %fusion.4 = f32[2048,512]{1,0:T(8,128)S(1)} fusion(bf16[2048,512]{1,0:T(8,128)(2,1)S(1)} %bitcast.75, bf16[2048,8192]{1,0:T(8,128)(2,1)} %param.5, s32[]{:T(128)S(6)} %select_n.365), kind=kOutput, calls=%fused_computation.4 | convolution fusion | flops 4294967296 | bytes 14680068 | tf_op jit(solution)/shard_map/dot_general | solution.py:12
  226.8 11.7 %custom-call.12 = f32[128,128]{1,0:T(8,128)S(1)} custom-call(f32[128,128]{1,0:T(8,128)S(1)} %slice.68), custom_call_target="Cholesky" | custom-call | tf_op jit(solution)/shard_map/cholesky/custom-call.1 | solution.py:59
  239.9 9.8 %custom-call.13 = f32[1,128,128]{1,2,0:T(8,128)S(1)} custom-call(f32[1,128,128]{2,1,0:T(8,128)S(1)} %fusion.70), custom_call_target="InvertDiagBlocksLowerTriangular" | custom-call | tf_op jit(solution)/shard_map/triangular_solve/custom-call.0 | solution.py:60
  251.9 11.7 %custom-call.14 = f32[128,128]{1,0:T(8,128)S(1)} custom-call(f32[128,128]{1,0:T(8,128)S(1)} %slice.71), custom_call_target="Cholesky" | custom-call | tf_op jit(solution)/shard_map/cholesky/custom-call.1 | solution.py:59
  265.0 10.2 %custom-call.15 = f32[1,128,128]{1,2,0:T(8,128)S(1)} custom-call(f32[1,128,128]{2,1,0:T(8,128)S(1)} %fusion.71), custom_call_target="InvertDiagBlocksLowerTriangular" | custom-call | tf_op jit(solution)/shard_map/triangular_solve/custom-call.0 | solution.py:60
  278.1 12.3 %custom-call.16 = f32[128,128]{1,0:T(8,128)} custom-call(f32[128,128]{1,0:T(8,128)S(1)} %slice.75), custom_call_target="Cholesky" | custom-call | tf_op jit(solution)/shard_map/cholesky/custom-call.1 | solution.py:59
  297.0 11.3 %custom-call.17 = f32[1,128,128]{1,2,0:T(8,128)} custom-call(f32[1,128,128]{2,1,0:T(8,128)} %fusion.72), custom_call_target="InvertDiagBlocksLowerTriangular" | custom-call | tf_op jit(solution)/shard_map/triangular_solve/custom-call.0 | solution.py:60
  313.5 13.2 %custom-call.18 = f32[128,128]{1,0:T(8,128)} custom-call(f32[128,128]{1,0:T(8,128)} %convolution_subtract_fusion.1), custom_call_target="Cholesky" | custom-call | tf_op jit(solution)/shard_map/cholesky/custom-call.1 | solution.py:59
  326.7 3.7 add_convert_fusion.1
  331.8 9.8 %custom-call.19 = f32[1,128,128]{1,2,0:T(8,128)S(1)} custom-call(f32[1,128,128]{2,1,0:T(8,128)S(1)} %fusion.73), custom_call_target="InvertDiagBlocksLowerTriangular" | custom-call | tf_op jit(solution)/shard_map/triangular_solve/custom-call.0 | solution.py:60
  342.2 15.0 %collective-permute-done.27 = bf16[1024,512]{1,0:T(8,128)(2,1)} collective-permute-done((bf16[1024,512]{1,0:T(8,128)(2,1)}, bf16[1024,512]{1,0:T(8,128)(2,1)}, u32[]{:S(2)}, u32[]{:S(2)}) %collective-permute-start.27) | collective-permute-done | bytes 1048608 | tf_op jit(solution)/shard_map/ppermute | solution.py:131
  357.3 3.6 add_convert_fusion
  363.5 4.0 %convolution_convert_fusion = bf16[512,512]{1,0:T(8,128)(2,1)} fusion(bf16[512,512]{1,0:T(8,128)(2,1)} %collective-permute-done.8, f32[2,512,512]{2,1,0:T(8,128)S(1)} %bitcast_add_fusion, s32[]{:T(128)S(6)} %select_n.319, f32[128,128]{1,0:T(8,128)S(1)} %copy.7, f32[128,384]{1,0:T(8,128)S(1)} %convolution_negate_fusion, f32[128,128]{1,0:T(8,128)S(1)} %broadcast.69, ...), kind=kOutput, calls=%fused_computation.45 | convolution fusion | flops 1613496320 | bytes 3145732 | tf_op jit(solution)/shard_map/dot_general | solution.py:12
  367.5 19.6 %collective-permute-done.28 = bf16[1024,512]{1,0:T(8,128)(2,1)} collective-permute-done((bf16[1024,512]{1,0:T(8,128)(2,1)}, bf16[1024,512]{1,0:T(8,128)(2,1)}, u32[]{:S(2)}, u32[]{:S(2)}) %collective-permute-start.28) | collective-permute-done | bytes 1048608 | tf_op jit(solution)/shard_map/ppermute | solution.py:131
  387.1 6.2 %multiply_convert_fusion = bf16[1024,512]{1,0:T(8,128)(2,1)} fusion(bf16[1024,512]{1,0:T(8,128)(2,1)} %collective-permute-done.28, bf16[1024,512]{1,0:T(8,128)(2,1)} %collective-permute-done.22, f32[2048,512]{1,0:T(8,128)S(1)} %copy-done.14, s32[]{:T(128)S(6)} %select_n.362, f32[128,128]{1,0:T(8,128)S(1)} %copy.7, ...), kind=kOutput, calls=%fused_computation.30 | convolution fusion | flops 3226468352 | bytes 6291460 | tf_op jit(solution)/shard_map/dot_general | solution.py:12
  (157 shorter events, 74.7 us)
Async XLA Ops:
  0.6 28.5 %collective-permute-start.1 = (bf16[1024,512]{1,0:T(8,128)(2,1)}, bf16[1024,512]{1,0:T(8,128)(2,1)S(1)}, u32[]{:S(2)}, u32[]{:S(2)}) collective-permute-start(bf16[1024,512]{1,0:T(8,128)(2,1)} %param.6), channel_id=1, source_target_pairs={{0,8},{4,12},{8,16},{12,20},{16,24},{20,28},{24,0},{28,4},{1,9},{5... | collective-permute-start | bytes 3145736 | tf_op jit(solution)/shard_map/ppermute | solution.py:84
  3.7 26.9 %collective-permute-start = (bf16[1024,512]{1,0:T(8,128)(2,1)}, bf16[1024,512]{1,0:T(8,128)(2,1)S(1)}, u32[]{:S(2)}, u32[]{:S(2)}) collective-permute-start(bf16[1024,512]{1,0:T(8,128)(2,1)} %param.6), channel_id=1, source_target_pairs={{0,4},{4,0},{8,12},{12,8},{16,20},{20,16},{24,28},{28,24},{1,5},{5... | collective-permute-start | bytes 3145736 | tf_op jit(solution)/shard_map/ppermute | solution.py:83
  29.1 27.9 %collective-permute-start.2 = (bf16[1024,512]{1,0:T(8,128)(2,1)S(1)}, bf16[1024,512]{1,0:T(8,128)(2,1)S(1)}, u32[]{:S(2)}, u32[]{:S(2)}) collective-permute-start(bf16[1024,512]{1,0:T(8,128)(2,1)S(1)} %collective-permute-done.1), channel_id=1, source_target_pairs={{0,4},{4,0},{8,12},{12,8},{16,20},{20,16},{24,28},{28,24},{1,5},{5... | collective-permute-start | bytes 3145736 | tf_op jit(solution)/shard_map/ppermute | solution.py:83
  30.6 25.6 %collective-permute-start.3 = (bf16[1024,512]{1,0:T(8,128)(2,1)S(1)}, bf16[1024,512]{1,0:T(8,128)(2,1)S(1)}, u32[]{:S(2)}, u32[]{:S(2)}) collective-permute-start(bf16[1024,512]{1,0:T(8,128)(2,1)S(1)} %collective-permute-done.1), channel_id=1, source_target_pairs={{0,8},{4,12},{8,16},{12,20},{16,24},{20,28},{24,0},{28,4},{1,9},{5... | collective-permute-start | bytes 3145736 | tf_op jit(solution)/shard_map/ppermute | solution.py:84
  56.2 22.9 %collective-permute-start.4 = (bf16[1024,512]{1,0:T(8,128)(2,1)S(1)}, bf16[1024,512]{1,0:T(8,128)(2,1)S(1)}, u32[]{:S(2)}, u32[]{:S(2)}) collective-permute-start(bf16[1024,512]{1,0:T(8,128)(2,1)S(1)} %collective-permute-done.3), channel_id=1, source_target_pairs={{0,4},{4,0},{8,12},{12,8},{16,20},{20,16},{24,28},{28,24},{1,5},{5... | collective-permute-start | bytes 3145736 | tf_op jit(solution)/shard_map/ppermute | solution.py:83
  57.0 24.7 %collective-permute-start.5 = (bf16[1024,512]{1,0:T(8,128)(2,1)S(1)}, bf16[1024,512]{1,0:T(8,128)(2,1)S(1)}, u32[]{:S(2)}, u32[]{:S(2)}) collective-permute-start(bf16[1024,512]{1,0:T(8,128)(2,1)S(1)} %collective-permute-done.3), channel_id=1, source_target_pairs={{0,8},{4,12},{8,16},{12,20},{16,24},{20,28},{24,0},{28,4},{1,9},{5... | collective-permute-start | bytes 3145736 | tf_op jit(solution)/shard_map/ppermute | solution.py:84
  81.7 21.9 %collective-permute-start.6 = (bf16[1024,512]{1,0:T(8,128)(2,1)S(1)}, bf16[1024,512]{1,0:T(8,128)(2,1)S(1)}, u32[]{:S(2)}, u32[]{:S(2)}) collective-permute-start(bf16[1024,512]{1,0:T(8,128)(2,1)S(1)} %collective-permute-done.5), channel_id=1, source_target_pairs={{0,4},{4,0},{8,12},{12,8},{16,20},{20,16},{24,28},{28,24},{1,5},{5... | collective-permute-start | bytes 3145736 | tf_op jit(solution)/shard_map/ppermute | solution.py:83
  118.7 4.4 %collective-permute-start.7 = (f32[2,512,512]{2,1,0:T(8,128)S(1)}, f32[2,512,512]{2,1,0:T(8,128)}, u32[]{:S(2)}, u32[]{:S(2)}) collective-permute-start(f32[2,512,512]{2,1,0:T(8,128)S(1)} %dynamic-slice_bitcast_fusion), channel_id=1, source_target_pairs={{0,1},{1,0},{2,3},{3,2},{4,5},{5,4},{6,7},{7,6},{8,9},{9,8},{10,11... | collective-permute-start | bytes 6291464 | tf_op jit(solution)/shard_map/ppermute | solution.py:99
  125.8 14.1 %collective-permute-start.8 = (bf16[512,512]{1,0:T(8,128)(2,1)S(1)}, bf16[512,512]{1,0:T(8,128)(2,1)}, u32[]{:S(2)}, u32[]{:S(2)}) collective-permute-start(bf16[512,512]{1,0:T(8,128)(2,1)S(1)} %fusion.45), channel_id=1, source_target_pairs={{0,2},{1,3},{2,0},{3,1},{4,6},{5,7},{6,4},{7,5},{8,10},{9,11},{10,... | collective-permute-start | bytes 1572872 | tf_op jit(solution)/shard_map/ppermute | solution.py:106
  143.9 2.3 collective-permute-start.9
  148.1 8.4 %collective-permute-start.10 = (f32[128,512]{1,0:T(8,128)S(1)}, f32[128,512]{1,0:T(8,128)S(1)}, u32[]{:S(2)}, u32[]{:S(2)}) collective-permute-start(f32[128,512]{1,0:T(8,128)S(1)} %constant_dynamic-slice_fusion.3), channel_id=1, source_target_pairs={{0,2},{1,3},{2,0},{3,1},{4,6},{5,7},{6,4},{7,5},{8,10},{9,11},{10,... | collective-permute-start | bytes 786440 | tf_op jit(solution)/shard_map/ppermute | solution.py:37
  157.5 5.1 %collective-permute-start.11 = (f32[64,512]{1,0:T(8,128)S(1)}, f32[64,512]{1,0:T(8,128)}, u32[]{:S(2)}, u32[]{:S(2)}) collective-permute-start(f32[64,512]{1,0:T(8,128)S(1)} %constant_dynamic-slice_fusion.2), channel_id=1, source_target_pairs={{0,4},{4,0},{8,12},{12,8},{16,20},{20,16},{24,28},{28,24},{1,5},{5... | collective-permute-start | bytes 393224 | tf_op jit(solution)/shard_map/ppermute | solution.py:37
  159.6 12.9 %collective-permute-start.20 = (bf16[512,512]{1,0:T(8,128)(2,1)S(1)}, bf16[512,512]{1,0:T(8,128)(2,1)S(1)}, u32[]{:S(2)}, u32[]{:S(2)}) collective-permute-start(bf16[512,512]{1,0:T(8,128)(2,1)S(1)} %fusion.46), channel_id=1, source_target_pairs={{0,2},{1,3},{2,0},{3,1},{4,6},{5,7},{6,4},{7,5},{8,10},{9,11},{10,... | collective-permute-start | bytes 1572872 | tf_op jit(solution)/shard_map/ppermute | solution.py:112
  161.1 11.5 %collective-permute-start.19 = (bf16[512,512]{1,0:T(8,128)(2,1)S(1)}, bf16[512,512]{1,0:T(8,128)(2,1)}, u32[]{:S(2)}, u32[]{:S(2)}) collective-permute-start(bf16[512,512]{1,0:T(8,128)(2,1)S(1)} %fusion.46), channel_id=1, source_target_pairs={{0,1},{1,0},{2,3},{3,2},{4,5},{5,4},{6,7},{7,6},{8,9},{9,8},{10,11... | collective-permute-start | bytes 1572872 | tf_op jit(solution)/shard_map/ppermute | solution.py:111
  163.6 8.9 %collective-permute-start.12 = (f32[32,512]{1,0:T(8,128)S(1)}, f32[32,512]{1,0:T(8,128)S(1)}, u32[]{:S(2)}, u32[]{:S(2)}) collective-permute-start(f32[32,512]{1,0:T(8,128)S(1)} %constant_dynamic-slice_fusion.1), channel_id=1, source_target_pairs={{0,8},{4,12},{8,0},{12,4},{16,24},{20,28},{24,16},{28,20},{1,9},{5... | collective-permute-start | bytes 196616 | tf_op jit(solution)/shard_map/ppermute | solution.py:37
  172.5 9.8 %collective-permute-start.21 = (bf16[512,512]{1,0:T(8,128)(2,1)S(1)}, bf16[512,512]{1,0:T(8,128)(2,1)S(1)}, u32[]{:S(2)}, u32[]{:S(2)}) collective-permute-start(bf16[512,512]{1,0:T(8,128)(2,1)S(1)} %collective-permute-done.20), channel_id=1, source_target_pairs={{0,1},{1,0},{2,3},{3,2},{4,5},{5,4},{6,7},{7,6},{8,9},{9,8},{10,11... | collective-permute-start | bytes 1572872 | tf_op jit(solution)/shard_map/ppermute | solution.py:111
  172.6 4.9 %collective-permute-start.13 = (f32[16,512]{1,0:T(8,128)S(1)}, f32[16,512]{1,0:T(8,128)S(1)}, u32[]{:S(2)}, u32[]{:S(2)}) collective-permute-start(f32[16,512]{1,0:T(8,128)S(1)} %constant_dynamic-slice_fusion), channel_id=1, source_target_pairs={{0,16},{4,20},{8,24},{12,28},{16,0},{20,4},{24,8},{28,12},{1,17},{... | collective-permute-start | bytes 98312 | tf_op jit(solution)/shard_map/ppermute | solution.py:37
  177.4 4.8 %collective-permute-start.14 = (f32[16,512]{1,0:T(8,128)S(1)}, f32[16,512]{1,0:T(8,128)S(1)}, u32[]{:S(2)}, u32[]{:S(2)}) collective-permute-start(f32[16,512]{1,0:T(8,128)S(1)} %dynamic-slice_add_fusion.4), channel_id=1, source_target_pairs={{0,16},{4,20},{8,24},{12,28},{16,0},{20,4},{24,8},{28,12},{1,17},{... | collective-permute-start | bytes 98312 | tf_op jit(solution)/shard_map/ppermute | solution.py:42
  182.3 15.7 %collective-permute-start.15 = (f32[32,512]{1,0:T(8,128)S(1)}, f32[32,512]{1,0:T(8,128)S(1)}, u32[]{:S(2)}, u32[]{:S(2)}) collective-permute-start(f32[32,512]{1,0:T(8,128)S(1)} %pad_maximum_fusion.18), channel_id=1, source_target_pairs={{0,8},{4,12},{8,0},{12,4},{16,24},{20,28},{24,16},{28,20},{1,9},{5... | collective-permute-start | bytes 196616 | tf_op jit(solution)/shard_map/ppermute | solution.py:42
  189.5 35.4 %copy-start.13 = (f32[2048,512]{1,0:T(8,128)}, f32[2048,512]{1,0:T(8,128)S(1)}, u32[]{:S(2)}) copy-start(f32[2048,512]{1,0:T(8,128)S(1)} %fusion.12) | copy-start | bytes 12582916
  198.0 6.4 %collective-permute-start.16 = (f32[64,512]{1,0:T(8,128)S(1)}, f32[64,512]{1,0:T(8,128)S(1)}, u32[]{:S(2)}, u32[]{:S(2)}) collective-permute-start(f32[64,512]{1,0:T(8,128)S(1)} %pad_maximum_fusion.17), channel_id=1, source_target_pairs={{0,4},{4,0},{8,12},{12,8},{16,20},{20,16},{24,28},{28,24},{1,5},{5... | collective-permute-start | bytes 393224 | tf_op jit(solution)/shard_map/ppermute | solution.py:42
  200.4 90.0 %collective-permute-start.25 = (bf16[1024,512]{1,0:T(8,128)(2,1)}, bf16[1024,512]{1,0:T(8,128)(2,1)}, u32[]{:S(2)}, u32[]{:S(2)}) collective-permute-start(bf16[1024,512]{1,0:T(8,128)(2,1)} %dynamic-slice_convert_fusion), channel_id=1, source_target_pairs={{0,4},{4,0},{8,12},{12,8},{16,20},{20,16},{24,28},{28,24},{1,5},{5... | collective-permute-start | bytes 3145736 | tf_op jit(solution)/shard_map/ppermute | solution.py:127
  204.5 10.3 %collective-permute-start.17 = (f32[128,512]{1,0:T(8,128)S(1)}, f32[128,512]{1,0:T(8,128)S(1)}, u32[]{:S(2)}, u32[]{:S(2)}) collective-permute-start(f32[128,512]{1,0:T(8,128)S(1)} %pad_maximum_fusion.16), channel_id=1, source_target_pairs={{0,2},{1,3},{2,0},{3,1},{4,6},{5,7},{6,4},{7,5},{8,10},{9,11},{10,... | collective-permute-start | bytes 786440 | tf_op jit(solution)/shard_map/ppermute | solution.py:42
  214.3 112.5 %collective-permute-start.24 = (bf16[1024,512]{1,0:T(8,128)(2,1)}, bf16[1024,512]{1,0:T(8,128)(2,1)}, u32[]{:S(2)}, u32[]{:S(2)}) collective-permute-start(bf16[1024,512]{1,0:T(8,128)(2,1)} %dynamic-slice_convert_fusion.1), channel_id=1, source_target_pairs={{0,4},{4,0},{8,12},{12,8},{16,20},{20,16},{24,28},{28,24},{1,5},{5... | collective-permute-start | bytes 3145736 | tf_op jit(solution)/shard_map/ppermute | solution.py:127
  214.9 11.6 %collective-permute-start.18 = (f32[256,512]{1,0:T(8,128)S(1)}, f32[256,512]{1,0:T(8,128)S(1)}, u32[]{:S(2)}, u32[]{:S(2)}) collective-permute-start(f32[256,512]{1,0:T(8,128)S(1)} %pad_maximum_fusion.9), channel_id=1, source_target_pairs={{0,1},{1,0},{2,3},{3,2},{4,5},{5,4},{6,7},{7,6},{8,9},{9,8},{10,11... | collective-permute-start | bytes 1572872 | tf_op jit(solution)/shard_map/ppermute | solution.py:42
  223.4 118.8 %collective-permute-start.23 = (bf16[1024,512]{1,0:T(8,128)(2,1)}, bf16[1024,512]{1,0:T(8,128)(2,1)}, u32[]{:S(2)}, u32[]{:S(2)}) collective-permute-start(bf16[1024,512]{1,0:T(8,128)(2,1)} %dynamic-slice_convert_fusion.2), channel_id=1, source_target_pairs={{0,4},{4,0},{8,12},{12,8},{16,20},{20,16},{24,28},{28,24},{1,5},{5... | collective-permute-start | bytes 3145736 | tf_op jit(solution)/shard_map/ppermute | solution.py:127
  226.0 141.4 %collective-permute-start.22 = (bf16[1024,512]{1,0:T(8,128)(2,1)}, bf16[1024,512]{1,0:T(8,128)(2,1)}, u32[]{:S(2)}, u32[]{:S(2)}) collective-permute-start(bf16[1024,512]{1,0:T(8,128)(2,1)} %dynamic-slice_convert_fusion.3), channel_id=1, source_target_pairs={{0,4},{4,0},{8,12},{12,8},{16,20},{20,16},{24,28},{28,24},{1,5},{5... | collective-permute-start | bytes 3145736 | tf_op jit(solution)/shard_map/ppermute | solution.py:127
  292.8 34.0 %collective-permute-start.26 = (bf16[1024,512]{1,0:T(8,128)(2,1)S(1)}, bf16[1024,512]{1,0:T(8,128)(2,1)}, u32[]{:S(2)}, u32[]{:S(2)}) collective-permute-start(bf16[1024,512]{1,0:T(8,128)(2,1)S(1)} %add_convert_fusion.2), channel_id=1, source_target_pairs={{0,8},{4,12},{8,16},{12,20},{16,24},{20,28},{24,0},{28,4},{1,9},{5... | collective-permute-start | bytes 3145736 | tf_op jit(solution)/shard_map/ppermute | solution.py:131
  330.4 31.1 %copy-start.9 = (f32[128,128]{0,1:T(8,128)S(1)}, f32[128,128]{0,1:T(8,128)}, u32[]{:S(2)}) copy-start(f32[128,128]{0,1:T(8,128)} %copy-done.8) | copy-start | bytes 196612
  330.4 26.9 %collective-permute-start.27 = (bf16[1024,512]{1,0:T(8,128)(2,1)}, bf16[1024,512]{1,0:T(8,128)(2,1)}, u32[]{:S(2)}, u32[]{:S(2)}) collective-permute-start(bf16[1024,512]{1,0:T(8,128)(2,1)} %add_convert_fusion.1), channel_id=1, source_target_pairs={{0,8},{4,12},{8,16},{12,20},{16,24},{20,28},{24,0},{28,4},{1,9},{5... | collective-permute-start | bytes 3145736 | tf_op jit(solution)/shard_map/ppermute | solution.py:131
  331.8 30.7 %copy-start.12 = (f32[128,128]{0,1:T(8,128)S(1)}, f32[128,128]{0,1:T(8,128)}, u32[]{:S(2)}) copy-start(f32[128,128]{0,1:T(8,128)} %copy-done.11) | copy-start | bytes 196612
  360.9 26.2 %collective-permute-start.28 = (bf16[1024,512]{1,0:T(8,128)(2,1)}, bf16[1024,512]{1,0:T(8,128)(2,1)}, u32[]{:S(2)}, u32[]{:S(2)}) collective-permute-start(bf16[1024,512]{1,0:T(8,128)(2,1)} %add_convert_fusion), channel_id=1, source_target_pairs={{0,8},{4,12},{8,16},{12,20},{16,24},{20,28},{24,0},{28,4},{1,9},{5... | collective-permute-start | bytes 3145736 | tf_op jit(solution)/shard_map/ppermute | solution.py:131
  (14 other events, 109.1 us)

commit v2 on v1

--- a/solution.py
+++ b/solution.py
@@ -1,6 +1,8 @@
 import jax
 import jax.numpy as jnp
 from jax import lax
+from jax.experimental import pallas as pl
+from jax.experimental.pallas import tpu as pltpu
 from jax.sharding import PartitionSpec as P
 
 F32 = jnp.float32
@@ -46,29 +48,67 @@
     return held
 
 
+def inverse_kernel(gram_ref, out_ref, work_ref, aug_ref):
+    n, b, w = gram_ref.shape[0], 128, 4
+    work_ref[...] = gram_ref[...]
+    aug_ref[...] = (
+        lax.broadcasted_iota(jnp.int32, (n, n), 0) == lax.broadcasted_iota(jnp.int32, (n, n), 1)
+    ).astype(F32)
+    lane = lax.broadcasted_iota(jnp.int32, (8, b), 1)
+    sub = lax.broadcasted_iota(jnp.int32, (8, b), 0)
+
+    def block(i, carry):
+        at = pl.ds(pl.multiple_of(i * b, b), b)
+        x = [work_ref[pl.ds(pl.multiple_of(i * b + 8 * g, 8), 8), at] for g in range(b // 8)]
+        for base in range(0, b, w):
+            first = base // 8
+            groups = range(first, b // 8)
+            wide = {
+                (j, g): jnp.broadcast_to(x[g][:, j:j + 1], (8, b))
+                for j in range(base, base + w) for g in groups
+            }
+            for k in range(base, base + w):
+                s = k % 8
+                over = 1.0 / wide[k, first][s:s + 1]
+                row = jnp.where(lane[:1] == k, 1.0, x[first][s:s + 1]) * over
+                heads = {j: wide[j, first][s:s + 1] * over for j in range(k + 1, base + w)}
+                for g in groups:
+                    c = wide[k, g]
+                    gone = lane == k
+                    if g == first:
+                        c = jnp.where(sub > s, c, 0.0)
+                        gone = gone & (sub > s)
+                    x[g] = jnp.where(gone, 0.0, x[g]) - c * row
+                    for j, head in heads.items():
+                        wide[j, g] = wide[j, g] - c * head
+        rows = []
+        for g in range(b // 8):
+            here = lane == sub + 8 * g
+            pivot = jnp.sum(jnp.where(here, x[g], 0.0), axis=1, keepdims=True)
+            unit = jnp.where(lane < sub + 8 * g, x[g], jnp.where(here, 1.0, 0.0))
+            rows.append(unit / jnp.sqrt(pivot))
+        inv = jnp.concatenate(rows, 0)
+        head = dot(inv, work_ref[at, :], ((1,), (0,)), HIGH)
+        tail = dot(inv, aug_ref[at, :], ((1,), (0,)), HIGH)
+        out_ref[at, :] = tail
+        work_ref[...] -= dot(head, head, ((0,), (0,)), HIGH)
+        aug_ref[...] -= dot(head, tail, ((0,), (0,)), HIGH)
+        return carry
+
+    lax.fori_loop(0, n // b, block, 0)
+
+
 def inverse_factor(gram):
     n = gram.shape[0]
-    b = 128
-    eye = jnp.eye(b, dtype=F32)
-    rest = gram
-    rows = []
-    panels = []
-    count = n // b
-    for i in range(count):
-        head = rest[:b, :b]
-        low = lax.linalg.cholesky(head, symmetrize_input=False)
-        inv = lax.linalg.triangular_solve(low, eye, left_side=True, lower=True)
-        if i + 1 < count:
-            panel = dot(rest[b:, :b], inv, ((1,), (1,)), HIGH)
-            rest = rest[b:, b:] - dot(panel, panel, ((1,), (1,)), HIGH)
-            panels.append(panel)
-        left = jnp.zeros((b, i * b), F32)
-        if i:
-            own = jnp.concatenate([panels[j][(i - 1 - j) * b:(i - j) * b] for j in range(i)], 1)
-            left = -dot(inv, dot(own, jnp.concatenate(rows, 0)[:, :i * b], ((1,), (0,)), HIGH),
-                        ((1,), (0,)), HIGH)
-        rows.append(jnp.concatenate([left, inv, jnp.zeros((b, n - (i + 1) * b), F32)], 1))
-    return jnp.concatenate(rows, 0)
+    return pl.pallas_call(
+        inverse_kernel,
+        out_shape=jax.ShapeDtypeStruct((n, n), F32),
+        in_specs=[pl.BlockSpec(memory_space=pltpu.VMEM)],
+        out_specs=pl.BlockSpec(memory_space=pltpu.VMEM),
+        scratch_shapes=[pltpu.VMEM((n, n), F32), pltpu.VMEM((n, n), F32)],
+        cost_estimate=pl.CostEstimate(flops=20_000_000_000, bytes_accessed=8 * n * n, transcendentals=0),
+        compiler_params=pltpu.CompilerParams(vmem_limit_bytes=24 * 2**20),
+    )(gram)
 
 
 def per_device(n_row, n_col, d, weight, basis_prev):
@@ -76,6 +116,7 @@
     me = lax.axis_index("row")
     group, side = me // 2, me % 2
     ring = n_row // 2
+    down_ring = [(j, i) for i, j in ring_of(n_row)]
 
     held = basis_prev
     partial = None
@@ -83,10 +124,18 @@
         other = lax.ppermute(held, "row", pair_of(n_row))
         later = lax.ppermute(held, "row", ring_of(n_row)) if step + 1 < ring else None
         owner = (group - step + ring) % ring
-        both = jnp.concatenate([jnp.where(side == 0, held, other), jnp.where(side == 0, other, held)], 0)
-        cut = lax.dynamic_slice_in_dim(weight, owner * 2 * depth, 2 * depth, 1)
-        term = dot(cut, both, ((1,), (0,)))
-        partial = term if partial is None else partial + term
+        if step + 1 < ring:
+            both = jnp.concatenate(
+                [jnp.where(side == 0, held, other), jnp.where(side == 0, other, held)], 0)
+            cut = lax.dynamic_slice_in_dim(weight, owner * 2 * depth, 2 * depth, 1)
+            term = dot(cut, both, ((1,), (0,)))
+            partial = term if partial is None else partial + term
+        else:
+            cut = lax.dynamic_slice_in_dim(weight, (owner * 2 + side) * depth, depth, 1)
+            partial = partial + dot(cut, held, ((1,), (0,)))
+            partial, other = lax.optimization_barrier((partial, other))
+            cut = lax.dynamic_slice_in_dim(weight, (owner * 2 + 1 - side) * depth, depth, 1)
+            partial = partial + dot(cut, other, ((1,), (0,)))
         held = later
 
     rows = weight.shape[0] // n_col
@@ -116,19 +165,43 @@
     full = full.reshape(n_col * rows, rank)
 
     gram = dot(sketch, sketch, ((0,), (0,)), HIGH)
-    gram = all_sum(gram, (("col", n_col), ("row", n_row)))
+    full, gram = lax.optimization_barrier((full, gram))
+    gram = all_sum(gram, (("row", n_row), ("col", n_col)))
     inverse = inverse_factor(gram / F32(d))
 
-    factor = None
-    for step in range(ring):
-        at = (group - 1 - step + 2 * ring) % ring
+    def factor_of(at):
         cut = lax.dynamic_slice_in_dim(weight, at * 2 * depth, 2 * depth, 1)
         term = dot(cut, full, ((0,), (0,)))
-        got = lax.ppermute(rows_of(term, (1 - side) * depth, depth).astype(BF16), "row", pair_of(n_row))
-        term = rows_of(term, side * depth, depth) + got.astype(F32)
-        factor = term if factor is None else term + factor.astype(F32)
-        if step + 1 < ring:
-            factor = lax.ppermute(factor.astype(BF16), "row", ring_of(n_row))
+        away = rows_of(term, (1 - side) * depth, depth).astype(BF16)
+        return rows_of(term, side * depth, depth), lax.ppermute(away, "row", pair_of(n_row))
+
+    up_hops = ring // 2
+    down_hops = ring - 1 - up_hops
+    order = []
+    for step in range(up_hops):
+        order.append(up_hops - step)
+        if step < down_hops:
+            order.append(step - down_hops)
+    order.append(0)
+    terms = {at: factor_of((group + at + ring) % ring) for at in order}
+
+    def travel(hops, sign, pairs):
+        moving = None
+        for step in range(hops):
+            own, got = terms[sign * (hops - step)]
+            own = own + got.astype(F32)
+            if moving is not None:
+                own = own + moving.astype(F32)
+            moving = lax.ppermute(own.astype(BF16), "row", pairs)
+        return moving
+
+    up = travel(up_hops, 1, ring_of(n_row))
+    down = travel(down_hops, -1, down_ring)
+    factor, got = terms[0]
+    factor = factor + got.astype(F32)
+    for moved in (up, down):
+        if moved is not None:
+            factor = factor + moved.astype(F32)
 
     left_basis = dot(sketch, inverse, ((1,), (1,)), HIGH).astype(BF16)
     right = dot(factor, inverse, ((1,), (1,)), HIGH)

time: 401 us -> 318 us (0.79); the launches traced: 393 us -> 317 us
  other arithmetic: 116 us -> 12.3 us
  Pallas kernels: 0 us -> 27.6 us
  waiting for transfers between devices: 153 us -> 179 us
  matrix products: 89.4 us -> 69.4 us
  local copies, waits for them, and re-layouts: 11.3 us -> 4.36 us
    another operation x20 -> x0, other arithmetic: 96 us -> none  [the longest x12 51.7 us: inverse_factor(): low = lax.linalg.cholesky(head, symmetrize_input=False)]
    ppermute x5, waiting for transfers between devices: 7.29 us -> 40.6 us  [all_sum(): got = lax.ppermute(held, axis, pairs)]
    pallas_call x0 -> x1, Pallas kernels: none -> 27.6 us  [inverse_factor(): pl.pallas_call(inverse_kernel, out_shape=jax.ShapeDtypeStruct((n, n), F32...]
    dot_general x23 -> x12, matrix products: 87.5 us -> 69.4 us  [dot(): lax.dot_general(a, b, ((dims[0], dims[1]), ((), ())), precision=precision...]
    ppermute x7, waiting for transfers between devices: 34.6 us -> 18.4 us  [the longest x4 13.4 us: factor_of(): lax.ppermute(away, 'row', pair_of(n_row))]
    convert_element_type x3, other arithmetic: 9.6 us -> 1.17 us  [travel(): moving = lax.ppermute(own.astype(BF16), 'row', pairs)]
    ppermute x5, waiting for transfers between devices: 15 us -> 23 us  [all_sum(): got = lax.ppermute(rows_of(held, (1 - mine) * half, half), axis, pairs)]
    convert_element_type x4, local copies, waits for them, and re-layouts: 4.72 us -> 0.55 us  [factor_of(): away = rows_of(term, (1 - side) * depth, depth).astype(BF16)]
  transfers between devices with their start and end apart: 29 -> 29, of which waited for: 16 -> 17; matrix products, arithmetic and copies ran while one was open for 47% -> 21% of each run, Pallas kernels for 0% -> 9%
where the time goes in v2:
time: 318 us; the launch traced here: 317 us
  waiting for transfers between devices  179 us (56%)
  matrix products  69.4 us (22%)
  Pallas kernels  27.6 us (9%)
  starting transfers between devices  23.1 us (7%)
  other arithmetic  12.3 us (4%)
  local copies, waits for them, and re-layouts  4.36 us (1%)
    dot_general x12, matrix products, dot(): lax.dot_general(a, b, ((dims[0], dims[1]), ((), ())), precision=precision...  69.4 us
    ppermute x3, waiting for transfers between devices, per_device(): lax.ppermute(held, 'row', ring_of(n_row))  43.6 us
    ppermute x5, waiting for transfers between devices, all_sum(): got = lax.ppermute(held, axis, pairs)  40.6 us
    pallas_call x1, Pallas kernels, inverse_factor(): pl.pallas_call(inverse_kernel, out_shape=jax.ShapeDtypeStruct((n, n), F32...  27.6 us
    ppermute x4, waiting for transfers between devices, per_device(): other = lax.ppermute(held, 'row', pair_of(n_row))  23.8 us
    ppermute x5, waiting for transfers between devices, all_sum(): got = lax.ppermute(rows_of(held, (1 - mine) * half, half), axis, pairs)  23 us
    ppermute x4, waiting for transfers between devices, factor_of(): lax.ppermute(away, 'row', pair_of(n_row))  13.4 us
    ppermute x1, waiting for transfers between devices, per_device(): sketch = lax.ppermute(sketch.astype(BF16), 'col', ring_of(n_col))  13.2 us
  transfers between devices with their start and end apart: 29, of which 17 were waited for; matrix products, arithmetic and copies ran while one was open for 21% of the time, Pallas kernels for 9%

profile of v2, /device:TPU:0, one launch (start us, length us, event | category | flops | bytes accessed | tf_op | source)
XLA Modules:
  0.0 317.5 jit_solution(4429883453799029707)
XLA Ops:
  0.6 3.1 collective-permute-start.1
  5.2 23.9 %collective-permute-done.1 = bf16[1024,512]{1,0:T(8,128)(2,1)S(1)} collective-permute-done((bf16[1024,512]{1,0:T(8,128)(2,1)}, bf16[1024,512]{1,0:T(8,128)(2,1)S(1)}, u32[]{:S(2)}, u32[]{:S(2)}) %collective-permute-start.1) | collective-permute-done | bytes 1048608 | tf_op jit(solution)/shard_map/ppermute | solution.py:125
  32.0 6.9 %fusion.12 = f32[2048,512]{1,0:T(8,128)S(1)} fusion(bf16[2048,8192]{1,0:T(8,128)(2,1)} %param.2, s32[]{:T(128)S(6)} %select_n.276, bf16[1024,512]{1,0:T(8,128)(2,1)S(1)} %get-tuple-element.13, bf16[1024,512]{1,0:T(8,128)(2,1)S(1)} %get-tuple-element.12), kind=kOutput, calls=%fused_computation.12 | convolution fusion | flops 4299161600 | bytes 14680068 | tf_op jit(solution)/shard_map/dot_general | solution.py:14
  38.9 17.3 %collective-permute-done.3 = bf16[1024,512]{1,0:T(8,128)(2,1)S(1)} collective-permute-done((bf16[1024,512]{1,0:T(8,128)(2,1)S(1)}, bf16[1024,512]{1,0:T(8,128)(2,1)S(1)}, u32[]{:S(2)}, u32[]{:S(2)}) %collective-permute-start.3) | collective-permute-done | bytes 1048608 | tf_op jit(solution)/shard_map/ppermute | solution.py:125
  57.3 6.9 %fusion.8 = f32[2048,512]{1,0:T(8,128)S(1)} fusion(bf16[2048,8192]{1,0:T(8,128)(2,1)} %param.2, s32[]{:T(128)S(6)} %select_n.282, bf16[1024,512]{1,0:T(8,128)(2,1)S(1)} %get-tuple-element.11, bf16[1024,512]{1,0:T(8,128)(2,1)S(1)} %get-tuple-element.10), kind=kOutput, calls=%fused_computation.8 | convolution fusion | flops 4299161600 | bytes 14680068 | tf_op jit(solution)/shard_map/dot_general | solution.py:14
  64.2 15.0 %collective-permute-done.4 = bf16[1024,512]{1,0:T(8,128)(2,1)S(1)} collective-permute-done((bf16[1024,512]{1,0:T(8,128)(2,1)S(1)}, bf16[1024,512]{1,0:T(8,128)(2,1)S(1)}, u32[]{:S(2)}, u32[]{:S(2)}) %collective-permute-start.4) | collective-permute-done | bytes 1048608 | tf_op jit(solution)/shard_map/ppermute | solution.py:124
  79.3 2.4 collective-permute-done.5
  82.7 7.0 %fusion.4 = f32[2048,512]{1,0:T(8,128)S(1)} fusion(bf16[2048,8192]{1,0:T(8,128)(2,1)} %param.2, s32[]{:T(128)S(6)} %select_n.286, bf16[1024,512]{1,0:T(8,128)(2,1)S(1)} %get-tuple-element.15, bf16[1024,512]{1,0:T(8,128)(2,1)S(1)} %get-tuple-element.14), kind=kOutput, calls=%fused_computation.4 | convolution fusion | flops 4299161600 | bytes 14680068 | tf_op jit(solution)/shard_map/dot_general | solution.py:14
  89.7 5.0 %add_add_fusion = f32[2048,512]{1,0:T(8,128)S(1)} fusion(f32[2048,512]{1,0:T(8,128)S(1)} %fusion.4, f32[2048,512]{1,0:T(8,128)S(1)} %fusion.12, f32[2048,512]{1,0:T(8,128)S(1)} %fusion.8, bf16[1024,512]{1,0:T(8,128)(2,1)S(1)} %collective-permute-done.5, bf16[2048,8192]{1,0:T(8,128)(2,1)} %param.2, s32[]{:T(128)S(6)} %select_n.290), kind=kOutput, calls=%fused_computation.18 | convolution fusion | flops 2150629376 | bytes 22020100 | tf_op jit(solution)/shard_map/dot_general | solution.py:14
  94.8 8.8 %collective-permute-done.6 = bf16[1024,512]{1,0:T(8,128)(2,1)S(1)} collective-permute-done((bf16[1024,512]{1,0:T(8,128)(2,1)S(1)}, bf16[1024,512]{1,0:T(8,128)(2,1)S(1)}, u32[]{:S(2)}, u32[]{:S(2)}) %collective-permute-start.6) | collective-permute-done | bytes 1048608 | tf_op jit(solution)/shard_map/ppermute | solution.py:124
  103.6 4.6 %fusion.14 = f32[2048,512]{1,0:T(8,128)S(1)} fusion(bf16[1024,512]{1,0:T(8,128)(2,1)S(1)} %collective-permute-done.6, bf16[2048,8192]{1,0:T(8,128)(2,1)} %param.2, s32[]{:T(128)S(6)} %select_n.291), kind=kOutput, calls=%fused_computation.14 | convolution fusion | flops 2147483648 | bytes 9437188 | tf_op jit(solution)/shard_map/dot_general | solution.py:14
  109.2 2.0 copy-done
  111.5 4.2 %collective-permute-done.7 = f32[2,512,512]{2,1,0:T(8,128)} collective-permute-done((f32[2,512,512]{2,1,0:T(8,128)S(1)}, f32[2,512,512]{2,1,0:T(8,128)}, u32[]{:S(2)}, u32[]{:S(2)}) %collective-permute-start.7) | collective-permute-done | bytes 2097184 | tf_op jit(solution)/shard_map/ppermute | solution.py:148
  115.7 2.7 bitcast_add_fusion
  119.3 13.2 %collective-permute-done.8 = bf16[512,512]{1,0:T(8,128)(2,1)S(1)} collective-permute-done((bf16[512,512]{1,0:T(8,128)(2,1)S(1)}, bf16[512,512]{1,0:T(8,128)(2,1)S(1)}, u32[]{:S(2)}, u32[]{:S(2)}) %collective-permute-start.8) | collective-permute-done | bytes 524320 | tf_op jit(solution)/shard_map/ppermute | solution.py:155
  133.5 12.5 %collective-permute-done.10 = bf16[512,512]{1,0:T(8,128)(2,1)} collective-permute-done((bf16[512,512]{1,0:T(8,128)(2,1)S(1)}, bf16[512,512]{1,0:T(8,128)(2,1)}, u32[]{:S(2)}, u32[]{:S(2)}) %collective-permute-start.10) | collective-permute-done | bytes 524320 | tf_op jit(solution)/shard_map/ppermute | solution.py:161
  153.1 13.7 %collective-permute-done.12 = f32[256,512]{1,0:T(8,128)} collective-permute-done((f32[256,512]{1,0:T(8,128)S(1)}, f32[256,512]{1,0:T(8,128)}, u32[]{:S(2)}, u32[]{:S(2)}) %collective-permute-start.12) | collective-permute-done | bytes 524320 | tf_op jit(solution)/shard_map/ppermute | solution.py:39
  168.4 7.9 %collective-permute-done.13 = f32[128,512]{1,0:T(8,128)} collective-permute-done((f32[128,512]{1,0:T(8,128)S(1)}, f32[128,512]{1,0:T(8,128)}, u32[]{:S(2)}, u32[]{:S(2)}) %collective-permute-start.13) | collective-permute-done | bytes 262176 | tf_op jit(solution)/shard_map/ppermute | solution.py:39
  177.3 8.6 %fusion.6 = f32[2048,512]{1,0:T(8,128)S(1)} fusion(bf16[2048,512]{1,0:T(8,128)(2,1)} %bitcast.40, bf16[2048,8192]{1,0:T(8,128)(2,1)} %param.2, s32[]{:T(128)S(6)} %select_n.282), kind=kOutput, calls=%fused_computation.6 | convolution fusion | flops 4294967296 | bytes 14680068 | tf_op jit(solution)/shard_map/dot_general | solution.py:14
  186.0 7.2 %fusion = f32[2048,512]{1,0:T(8,128)S(1)} fusion(bf16[2048,512]{1,0:T(8,128)(2,1)S(1)} %bitcast.41, bf16[2048,8192]{1,0:T(8,128)(2,1)} %param.2, s32[]{:T(128)S(6)} %select_n.341), kind=kOutput, calls=%fused_computation | convolution fusion | flops 4294967296 | bytes 14680068 | tf_op jit(solution)/shard_map/dot_general | solution.py:14
  198.0 6.9 %fusion.2 = f32[2048,512]{1,0:T(8,128)S(1)} fusion(bf16[2048,512]{1,0:T(8,128)(2,1)S(1)} %bitcast.42, bf16[2048,8192]{1,0:T(8,128)(2,1)} %param.2, s32[]{:T(128)S(6)} %select_n.339), kind=kOutput, calls=%fused_computation.2 | convolution fusion | flops 4294967296 | bytes 14680068 | tf_op jit(solution)/shard_map/dot_general | solution.py:14
  206.8 2.0 collective-permute-start.19
  210.1 5.8 %collective-permute-done.19 = f32[64,512]{1,0:T(8,128)S(1)} collective-permute-done((f32[64,512]{1,0:T(8,128)S(1)}, f32[64,512]{1,0:T(8,128)S(1)}, u32[]{:S(2)}, u32[]{:S(2)}) %collective-permute-start.19) | collective-permute-done | bytes 131104 | tf_op jit(solution)/shard_map/ppermute | solution.py:44
  216.0 4.3 %collective-permute-done.24 = bf16[1024,512]{1,0:T(8,128)(2,1)S(1)} collective-permute-done((bf16[1024,512]{1,0:T(8,128)(2,1)S(1)}, bf16[1024,512]{1,0:T(8,128)(2,1)S(1)}, u32[]{:S(2)}, u32[]{:S(2)}) %collective-permute-start.24) | collective-permute-done | bytes 1048608 | tf_op jit(solution)/shard_map/ppermute | solution.py:176
  221.0 25.8 %collective-permute-done.20 = f32[128,512]{1,0:T(8,128)S(1)} collective-permute-done((f32[128,512]{1,0:T(8,128)S(1)}, f32[128,512]{1,0:T(8,128)S(1)}, u32[]{:S(2)}, u32[]{:S(2)}) %collective-permute-start.20) | collective-permute-done | bytes 262176 | tf_op jit(solution)/shard_map/ppermute | solution.py:44
  247.9 6.9 %fusion.10 = f32[2048,512]{1,0:T(8,128)S(1)} fusion(bf16[2048,512]{1,0:T(8,128)(2,1)S(1)} %bitcast.43, bf16[2048,8192]{1,0:T(8,128)(2,1)} %param.2, s32[]{:T(128)S(6)} %select_n.276), kind=kOutput, calls=%fused_computation.10 | convolution fusion | flops 4294967296 | bytes 14680068 | tf_op jit(solution)/shard_map/dot_general | solution.py:14
  256.1 9.2 %collective-permute-done.27 = bf16[1024,512]{1,0:T(8,128)(2,1)S(1)} collective-permute-done((bf16[1024,512]{1,0:T(8,128)(2,1)S(1)}, bf16[1024,512]{1,0:T(8,128)(2,1)S(1)}, u32[]{:S(2)}, u32[]{:S(2)}) %collective-permute-start.27) | collective-permute-done | bytes 1048608 | tf_op jit(solution)/shard_map/ppermute | solution.py:176
  267.4 9.1 %collective-permute-done.21 = f32[256,512]{1,0:T(8,128)S(1)} collective-permute-done((f32[256,512]{1,0:T(8,128)S(1)}, f32[256,512]{1,0:T(8,128)S(1)}, u32[]{:S(2)}, u32[]{:S(2)}) %collective-permute-start.21) | collective-permute-done | bytes 524320 | tf_op jit(solution)/shard_map/ppermute | solution.py:44
  277.5 27.6 %shard_map.41 = f32[512,512]{1,0:T(8,128)S(1)} custom-call(f32[512,512]{1,0:T(8,128)S(1)} %maximum_multiply_fusion.gram_ref), custom_call_target="tpu_custom_call" | custom-call | flops 20000000000 | bytes 2097152 | tf_op jit(solution)/shard_map/pallas_call | solution.py:103
  305.1 2.7 convolution_convert_fusion
  307.8 4.9 %collective-permute-done.26 = bf16[1024,512]{1,0:T(8,128)(2,1)S(1)} collective-permute-done((bf16[1024,512]{1,0:T(8,128)(2,1)S(1)}, bf16[1024,512]{1,0:T(8,128)(2,1)S(1)}, u32[]{:S(2)}, u32[]{:S(2)}) %collective-permute-start.26) | collective-permute-done | bytes 1048608 | tf_op jit(solution)/shard_map/ppermute | solution.py:195
  312.8 4.7 %multiply_convert_fusion = bf16[1024,512]{1,0:T(8,128)(2,1)} fusion(f32[512,512]{1,0:T(8,128)S(1)} %shard_map.41, bf16[1024,512]{1,0:T(8,128)(2,1)S(1)} %collective-permute-done.28, bf16[1024,512]{1,0:T(8,128)(2,1)S(1)} %collective-permute-done.26, bf16[1024,512]{1,0:T(8,128)(2,1)S(1)} %collective-permute-done.22, f32[2048,512]{1,0:T(8,128)S(1)} %fusion.10, ...), kind=kOutput, calls=%fused_computation.29 | convolution fusion | flops 3225419776 | bytes 7340036 | tf_op jit(solution)/shard_map/dot_general | solution.py:14
  (87 shorter events, 33.4 us)
Async XLA Ops:
  0.6 28.5 %collective-permute-start.1 = (bf16[1024,512]{1,0:T(8,128)(2,1)}, bf16[1024,512]{1,0:T(8,128)(2,1)S(1)}, u32[]{:S(2)}, u32[]{:S(2)}) collective-permute-start(bf16[1024,512]{1,0:T(8,128)(2,1)} %param.3), channel_id=1, source_target_pairs={{0,8},{4,12},{8,16},{12,20},{16,24},{20,28},{24,0},{28,4},{1,9},{5... | collective-permute-start | bytes 3145736 | tf_op jit(solution)/shard_map/ppermute | solution.py:125
  3.7 26.9 %collective-permute-start = (bf16[1024,512]{1,0:T(8,128)(2,1)}, bf16[1024,512]{1,0:T(8,128)(2,1)S(1)}, u32[]{:S(2)}, u32[]{:S(2)}) collective-permute-start(bf16[1024,512]{1,0:T(8,128)(2,1)} %param.3), channel_id=1, source_target_pairs={{0,4},{4,0},{8,12},{12,8},{16,20},{20,16},{24,28},{28,24},{1,5},{5... | collective-permute-start | bytes 3145736 | tf_op jit(solution)/shard_map/ppermute | solution.py:124
  29.1 27.9 %collective-permute-start.2 = (bf16[1024,512]{1,0:T(8,128)(2,1)S(1)}, bf16[1024,512]{1,0:T(8,128)(2,1)S(1)}, u32[]{:S(2)}, u32[]{:S(2)}) collective-permute-start(bf16[1024,512]{1,0:T(8,128)(2,1)S(1)} %collective-permute-done.1), channel_id=1, source_target_pairs={{0,4},{4,0},{8,12},{12,8},{16,20},{20,16},{24,28},{28,24},{1,5},{5... | collective-permute-start | bytes 3145736 | tf_op jit(solution)/shard_map/ppermute | solution.py:124
  30.6 25.6 %collective-permute-start.3 = (bf16[1024,512]{1,0:T(8,128)(2,1)S(1)}, bf16[1024,512]{1,0:T(8,128)(2,1)S(1)}, u32[]{:S(2)}, u32[]{:S(2)}) collective-permute-start(bf16[1024,512]{1,0:T(8,128)(2,1)S(1)} %collective-permute-done.1), channel_id=1, source_target_pairs={{0,8},{4,12},{8,16},{12,20},{16,24},{20,28},{24,0},{28,4},{1,9},{5... | collective-permute-start | bytes 3145736 | tf_op jit(solution)/shard_map/ppermute | solution.py:125
  56.2 22.9 %collective-permute-start.4 = (bf16[1024,512]{1,0:T(8,128)(2,1)S(1)}, bf16[1024,512]{1,0:T(8,128)(2,1)S(1)}, u32[]{:S(2)}, u32[]{:S(2)}) collective-permute-start(bf16[1024,512]{1,0:T(8,128)(2,1)S(1)} %collective-permute-done.3), channel_id=1, source_target_pairs={{0,4},{4,0},{8,12},{12,8},{16,20},{20,16},{24,28},{28,24},{1,5},{5... | collective-permute-start | bytes 3145736 | tf_op jit(solution)/shard_map/ppermute | solution.py:124
  57.0 24.7 %collective-permute-start.5 = (bf16[1024,512]{1,0:T(8,128)(2,1)S(1)}, bf16[1024,512]{1,0:T(8,128)(2,1)S(1)}, u32[]{:S(2)}, u32[]{:S(2)}) collective-permute-start(bf16[1024,512]{1,0:T(8,128)(2,1)S(1)} %collective-permute-done.3), channel_id=1, source_target_pairs={{0,8},{4,12},{8,16},{12,20},{16,24},{20,28},{24,0},{28,4},{1,9},{5... | collective-permute-start | bytes 3145736 | tf_op jit(solution)/shard_map/ppermute | solution.py:125
  81.7 21.9 %collective-permute-start.6 = (bf16[1024,512]{1,0:T(8,128)(2,1)S(1)}, bf16[1024,512]{1,0:T(8,128)(2,1)S(1)}, u32[]{:S(2)}, u32[]{:S(2)}) collective-permute-start(bf16[1024,512]{1,0:T(8,128)(2,1)S(1)} %collective-permute-done.5), channel_id=1, source_target_pairs={{0,4},{4,0},{8,12},{12,8},{16,20},{20,16},{24,28},{28,24},{1,5},{5... | collective-permute-start | bytes 3145736 | tf_op jit(solution)/shard_map/ppermute | solution.py:124
  109.2 2.0 copy-start
  111.4 4.4 %collective-permute-start.7 = (f32[2,512,512]{2,1,0:T(8,128)S(1)}, f32[2,512,512]{2,1,0:T(8,128)}, u32[]{:S(2)}, u32[]{:S(2)}) collective-permute-start(f32[2,512,512]{2,1,0:T(8,128)S(1)} %dynamic-slice_bitcast_fusion), channel_id=1, source_target_pairs={{0,1},{1,0},{2,3},{3,2},{4,5},{5,4},{6,7},{7,6},{8,9},{9,8},{10,11... | collective-permute-start | bytes 6291464 | tf_op jit(solution)/shard_map/ppermute | solution.py:148
  118.5 14.0 %collective-permute-start.8 = (bf16[512,512]{1,0:T(8,128)(2,1)S(1)}, bf16[512,512]{1,0:T(8,128)(2,1)S(1)}, u32[]{:S(2)}, u32[]{:S(2)}) collective-permute-start(bf16[512,512]{1,0:T(8,128)(2,1)S(1)} %fusion.39), channel_id=1, source_target_pairs={{0,2},{1,3},{2,0},{3,1},{4,6},{5,7},{6,4},{7,5},{8,10},{9,11},{10,... | collective-permute-start | bytes 1572872 | tf_op jit(solution)/shard_map/ppermute | solution.py:155
  132.7 13.3 %collective-permute-start.10 = (bf16[512,512]{1,0:T(8,128)(2,1)S(1)}, bf16[512,512]{1,0:T(8,128)(2,1)}, u32[]{:S(2)}, u32[]{:S(2)}) collective-permute-start(bf16[512,512]{1,0:T(8,128)(2,1)S(1)} %fusion.41), channel_id=1, source_target_pairs={{0,2},{1,3},{2,0},{3,1},{4,6},{5,7},{6,4},{7,5},{8,10},{9,11},{10,... | collective-permute-start | bytes 1572872 | tf_op jit(solution)/shard_map/ppermute | solution.py:161
  133.5 14.5 %collective-permute-start.9 = (bf16[512,512]{1,0:T(8,128)(2,1)S(1)}, bf16[512,512]{1,0:T(8,128)(2,1)}, u32[]{:S(2)}, u32[]{:S(2)}) collective-permute-start(bf16[512,512]{1,0:T(8,128)(2,1)S(1)} %fusion.41), channel_id=1, source_target_pairs={{0,1},{1,0},{2,3},{3,2},{4,5},{5,4},{6,7},{7,6},{8,9},{9,8},{10,11... | collective-permute-start | bytes 1572872 | tf_op jit(solution)/shard_map/ppermute | solution.py:160
  146.0 3.7 %collective-permute-start.11 = (bf16[512,512]{1,0:T(8,128)(2,1)}, bf16[512,512]{1,0:T(8,128)(2,1)S(1)}, u32[]{:S(2)}, u32[]{:S(2)}) collective-permute-start(bf16[512,512]{1,0:T(8,128)(2,1)} %collective-permute-done.10), channel_id=1, source_target_pairs={{0,1},{1,0},{2,3},{3,2},{4,5},{5,4},{6,7},{7,6},{8,9},{9,8},{10,11... | collective-permute-start | bytes 1572872 | tf_op jit(solution)/shard_map/ppermute | solution.py:160
  148.0 3.0 copy-start.1
  152.4 14.4 %collective-permute-start.12 = (f32[256,512]{1,0:T(8,128)S(1)}, f32[256,512]{1,0:T(8,128)}, u32[]{:S(2)}, u32[]{:S(2)}) collective-permute-start(f32[256,512]{1,0:T(8,128)S(1)} %constant_dynamic-slice_fusion.4), channel_id=1, source_target_pairs={{0,4},{4,0},{8,12},{12,8},{16,20},{20,16},{24,28},{28,24},{1,5},{5... | collective-permute-start | bytes 1572872 | tf_op jit(solution)/shard_map/ppermute | solution.py:39
  168.1 8.1 %collective-permute-start.13 = (f32[128,512]{1,0:T(8,128)S(1)}, f32[128,512]{1,0:T(8,128)}, u32[]{:S(2)}, u32[]{:S(2)}) collective-permute-start(f32[128,512]{1,0:T(8,128)S(1)} %constant_dynamic-slice_fusion.3), channel_id=1, source_target_pairs={{0,8},{4,12},{8,0},{12,4},{16,24},{20,28},{24,16},{28,20},{1,9},{5... | collective-permute-start | bytes 786440 | tf_op jit(solution)/shard_map/ppermute | solution.py:39
  177.2 8.8 %copy-start.3 = (bf16[2,2,512,512]{3,2,1,0:T(8,128)(2,1)S(1)}, bf16[2,2,512,512]{3,2,1,0:T(8,128)(2,1)}, u32[]{:S(2)}) copy-start(bf16[2,2,512,512]{3,2,1,0:T(8,128)(2,1)} %copy-done.2) | copy-start | bytes 6291460
  177.2 8.6 %collective-permute-start.14 = (f32[64,512]{1,0:T(8,128)S(1)}, f32[64,512]{1,0:T(8,128)S(1)}, u32[]{:S(2)}, u32[]{:S(2)}) collective-permute-start(f32[64,512]{1,0:T(8,128)S(1)} %constant_dynamic-slice_fusion.2), channel_id=1, source_target_pairs={{0,16},{4,20},{8,24},{12,28},{16,0},{20,4},{24,8},{28,12},{1,17},{... | collective-permute-start | bytes 393224 | tf_op jit(solution)/shard_map/ppermute | solution.py:39
  186.0 7.3 %collective-permute-start.15 = (f32[32,512]{1,0:T(8,128)S(1)}, f32[32,512]{1,0:T(8,128)S(1)}, u32[]{:S(2)}, u32[]{:S(2)}) collective-permute-start(f32[32,512]{1,0:T(8,128)S(1)} %constant_dynamic-slice_fusion.1), channel_id=1, source_target_pairs={{0,1},{1,0},{2,3},{3,2},{4,5},{5,4},{6,7},{7,6},{8,9},{9,8},{10,11... | collective-permute-start | bytes 196616 | tf_op jit(solution)/shard_map/ppermute | solution.py:39
  193.3 4.0 %collective-permute-start.16 = (f32[16,512]{1,0:T(8,128)S(1)}, f32[16,512]{1,0:T(8,128)S(1)}, u32[]{:S(2)}, u32[]{:S(2)}) collective-permute-start(f32[16,512]{1,0:T(8,128)S(1)} %constant_dynamic-slice_fusion), channel_id=1, source_target_pairs={{0,2},{1,3},{2,0},{3,1},{4,6},{5,7},{6,4},{7,5},{8,10},{9,11},{10,... | collective-permute-start | bytes 98312 | tf_op jit(solution)/shard_map/ppermute | solution.py:39
  194.2 26.1 %collective-permute-start.24 = (bf16[1024,512]{1,0:T(8,128)(2,1)S(1)}, bf16[1024,512]{1,0:T(8,128)(2,1)S(1)}, u32[]{:S(2)}, u32[]{:S(2)}) collective-permute-start(bf16[1024,512]{1,0:T(8,128)(2,1)S(1)} %dynamic-slice_convert_fusion.1), channel_id=1, source_target_pairs={{0,4},{4,0},{8,12},{12,8},{16,20},{20,16},{24,28},{28,24},{1,5},{5... | collective-permute-start | bytes 3145736 | tf_op jit(solution)/shard_map/ppermute | solution.py:176
  197.3 7.7 %collective-permute-start.17 = (f32[16,512]{1,0:T(8,128)S(1)}, f32[16,512]{1,0:T(8,128)S(1)}, u32[]{:S(2)}, u32[]{:S(2)}) collective-permute-start(f32[16,512]{1,0:T(8,128)S(1)} %dynamic-slice_add_fusion.4), channel_id=1, source_target_pairs={{0,2},{1,3},{2,0},{3,1},{4,6},{5,7},{6,4},{7,5},{8,10},{9,11},{10,... | collective-permute-start | bytes 98312 | tf_op jit(solution)/shard_map/ppermute | solution.py:44
  205.0 1.8 collective-permute-start.18
  205.2 71.5 %collective-permute-start.23 = (bf16[1024,512]{1,0:T(8,128)(2,1)S(1)}, bf16[1024,512]{1,0:T(8,128)(2,1)S(1)}, u32[]{:S(2)}, u32[]{:S(2)}) collective-permute-start(bf16[1024,512]{1,0:T(8,128)(2,1)S(1)} %dynamic-slice_convert_fusion.2), channel_id=1, source_target_pairs={{0,4},{4,0},{8,12},{12,8},{16,20},{20,16},{24,28},{28,24},{1,5},{5... | collective-permute-start | bytes 3145736 | tf_op jit(solution)/shard_map/ppermute | solution.py:176
  206.8 9.1 %collective-permute-start.19 = (f32[64,512]{1,0:T(8,128)S(1)}, f32[64,512]{1,0:T(8,128)S(1)}, u32[]{:S(2)}, u32[]{:S(2)}) collective-permute-start(f32[64,512]{1,0:T(8,128)S(1)} %pad_maximum_fusion.2), channel_id=1, source_target_pairs={{0,16},{4,20},{8,24},{12,28},{16,0},{20,4},{24,8},{28,12},{1,17},{... | collective-permute-start | bytes 393224 | tf_op jit(solution)/shard_map/ppermute | solution.py:44
  209.0 56.2 %collective-permute-start.27 = (bf16[1024,512]{1,0:T(8,128)(2,1)S(1)}, bf16[1024,512]{1,0:T(8,128)(2,1)S(1)}, u32[]{:S(2)}, u32[]{:S(2)}) collective-permute-start(bf16[1024,512]{1,0:T(8,128)(2,1)S(1)} %dynamic-slice_convert_fusion), channel_id=1, source_target_pairs={{0,4},{4,0},{8,12},{12,8},{16,20},{20,16},{24,28},{28,24},{1,5},{5... | collective-permute-start | bytes 3145736 | tf_op jit(solution)/shard_map/ppermute | solution.py:176
  215.9 30.8 %collective-permute-start.20 = (f32[128,512]{1,0:T(8,128)S(1)}, f32[128,512]{1,0:T(8,128)S(1)}, u32[]{:S(2)}, u32[]{:S(2)}) collective-permute-start(f32[128,512]{1,0:T(8,128)S(1)} %pad_maximum_fusion.1), channel_id=1, source_target_pairs={{0,8},{4,12},{8,0},{12,4},{16,24},{20,28},{24,16},{28,20},{1,9},{5... | collective-permute-start | bytes 786440 | tf_op jit(solution)/shard_map/ppermute | solution.py:44
  220.7 56.0 %collective-permute-start.25 = (bf16[1024,512]{1,0:T(8,128)(2,1)S(1)}, bf16[1024,512]{1,0:T(8,128)(2,1)S(1)}, u32[]{:S(2)}, u32[]{:S(2)}) collective-permute-start(bf16[1024,512]{1,0:T(8,128)(2,1)S(1)} %add_convert_fusion.2), channel_id=1, source_target_pairs={{0,8},{4,12},{8,16},{12,20},{16,24},{20,28},{24,0},{28,4},{1,9},{5... | collective-permute-start | bytes 3145736 | tf_op jit(solution)/shard_map/ppermute | solution.py:195
  246.8 29.6 %collective-permute-start.21 = (f32[256,512]{1,0:T(8,128)S(1)}, f32[256,512]{1,0:T(8,128)S(1)}, u32[]{:S(2)}, u32[]{:S(2)}) collective-permute-start(f32[256,512]{1,0:T(8,128)S(1)} %pad_maximum_fusion), channel_id=1, source_target_pairs={{0,4},{4,0},{8,12},{12,8},{16,20},{20,16},{24,28},{28,24},{1,5},{5... | collective-permute-start | bytes 1572872 | tf_op jit(solution)/shard_map/ppermute | solution.py:44
  255.0 52.9 %collective-permute-start.22 = (bf16[1024,512]{1,0:T(8,128)(2,1)S(1)}, bf16[1024,512]{1,0:T(8,128)(2,1)S(1)}, u32[]{:S(2)}, u32[]{:S(2)}) collective-permute-start(bf16[1024,512]{1,0:T(8,128)(2,1)S(1)} %dynamic-slice_convert_fusion.3), channel_id=1, source_target_pairs={{0,4},{4,0},{8,12},{12,8},{16,20},{20,16},{24,28},{28,24},{1,5},{5... | collective-permute-start | bytes 3145736 | tf_op jit(solution)/shard_map/ppermute | solution.py:176
  265.6 42.2 %collective-permute-start.28 = (bf16[1024,512]{1,0:T(8,128)(2,1)S(1)}, bf16[1024,512]{1,0:T(8,128)(2,1)S(1)}, u32[]{:S(2)}, u32[]{:S(2)}) collective-permute-start(bf16[1024,512]{1,0:T(8,128)(2,1)S(1)} %add_convert_fusion), channel_id=1, source_target_pairs={{8,0},{12,4},{16,8},{20,12},{24,16},{28,20},{0,24},{4,28},{9,1},{1... | collective-permute-start | bytes 3145736 | tf_op jit(solution)/shard_map/ppermute | solution.py:195
  277.2 35.6 %collective-permute-start.26 = (bf16[1024,512]{1,0:T(8,128)(2,1)S(1)}, bf16[1024,512]{1,0:T(8,128)(2,1)S(1)}, u32[]{:S(2)}, u32[]{:S(2)}) collective-permute-start(bf16[1024,512]{1,0:T(8,128)(2,1)S(1)} %add_convert_fusion.1), channel_id=1, source_target_pairs={{0,8},{4,12},{8,16},{12,20},{16,24},{20,28},{24,0},{28,4},{1,9},{5... | collective-permute-start | bytes 3145736 | tf_op jit(solution)/shard_map/ppermute | solution.py:195
  (1 other events, 1.4 us)

commit v3 on v2

--- a/solution.py
+++ b/solution.py
@@ -119,9 +119,15 @@
     down_ring = [(j, i) for i, j in ring_of(n_row)]
 
     held = basis_prev
-    partial = None
+    partial = other = None
+    half = depth // 2
     for step in range(ring):
-        other = lax.ppermute(held, "row", pair_of(n_row))
+        if step and step + 1 == ring:
+            first = lax.ppermute(held[:half], "row", pair_of(n_row))
+            second = lax.ppermute(other[half:], "row", ring_of(n_row))
+            other = jnp.concatenate([first, second], 0)
+        else:
+            other = lax.ppermute(held, "row", pair_of(n_row))
         later = lax.ppermute(held, "row", ring_of(n_row)) if step + 1 < ring else None
         owner = (group - step + ring) % ring
         if step + 1 < ring:
@@ -166,14 +172,12 @@
 
     gram = dot(sketch, sketch, ((0,), (0,)), HIGH)
     full, gram = lax.optimization_barrier((full, gram))
-    gram = all_sum(gram, (("row", n_row), ("col", n_col)))
+    gram = all_sum(gram, (("col", n_col), ("row", n_row)))
     inverse = inverse_factor(gram / F32(d))
 
-    def factor_of(at):
+    def term_of(at):
         cut = lax.dynamic_slice_in_dim(weight, at * 2 * depth, 2 * depth, 1)
-        term = dot(cut, full, ((0,), (0,)))
-        away = rows_of(term, (1 - side) * depth, depth).astype(BF16)
-        return rows_of(term, side * depth, depth), lax.ppermute(away, "row", pair_of(n_row))
+        return dot(cut, full, ((0,), (0,)))
 
     up_hops = ring // 2
     down_hops = ring - 1 - up_hops
@@ -183,13 +187,26 @@
         if step < down_hops:
             order.append(step - down_hops)
     order.append(0)
-    terms = {at: factor_of((group + at + ring) % ring) for at in order}
+    terms = {}
+    early = None
+    for at in order:
+        term = term_of((group + at + ring) % ring)
+        near = rows_of(term, side * depth, depth)
+        away = rows_of(term, (1 - side) * depth, depth)
+        if at == up_hops and at:
+            early = lax.ppermute(away[half:].astype(BF16), "row", ring_of(n_row))
+            got = lax.ppermute(away[:half].astype(BF16), "row", pair_of(n_row))
+            near = jnp.concatenate([near[:half] + got.astype(F32), near[half:]], 0)
+        else:
+            if at == up_hops - 1 and early is not None:
+                away = jnp.concatenate([away[:half], away[half:] + early.astype(F32)], 0)
+            near = near + lax.ppermute(away.astype(BF16), "row", pair_of(n_row)).astype(F32)
+        terms[at] = near
 
     def travel(hops, sign, pairs):
         moving = None
         for step in range(hops):
-            own, got = terms[sign * (hops - step)]
-            own = own + got.astype(F32)
+            own = terms[sign * (hops - step)]
             if moving is not None:
                 own = own + moving.astype(F32)
             moving = lax.ppermute(own.astype(BF16), "row", pairs)
@@ -197,8 +214,7 @@
 
     up = travel(up_hops, 1, ring_of(n_row))
     down = travel(down_hops, -1, down_ring)
-    factor, got = terms[0]
-    factor = factor + got.astype(F32)
+    factor = terms[0]
     for moved in (up, down):
         if moved is not None:
             factor = factor + moved.astype(F32)

time: 318 us -> 285 us (0.90)
  waiting for transfers between devices: 179 us -> 139 us
  starting transfers between devices: 23.1 us -> 32.1 us
    ppermute x4 -> x3, waiting for transfers between devices: 23.8 us -> 0.01 us  [per_device(): other = lax.ppermute(held, 'row', pair_of(n_row))]
    ppermute x5, waiting for transfers between devices: 40.6 us -> 27 us  [all_sum(): got = lax.ppermute(held, axis, pairs)]
    ppermute x3, waiting for transfers between devices: 43.6 us -> 57 us  [per_device(): lax.ppermute(held, 'row', ring_of(n_row))]
    ppermute x5, waiting for transfers between devices: 23 us -> 9.96 us  [all_sum(): got = lax.ppermute(rows_of(held, (1 - mine) * half, half), axis, pairs)]
    ppermute x5, starting transfers between devices: 1.79 us -> 9.15 us  [all_sum(): got = lax.ppermute(rows_of(held, (1 - mine) * half, half), axis, pairs)]
    ppermute x4 -> x7, waiting for transfers between devices: 13.4 us -> 12.4 us  [the longest x3 12 us: per_device(): lax.ppermute(away.astype(BF16), 'row', pair_of(n_row)).astype(F32)]
  transfers between devices with their start and end apart: 29 -> 31, of which waited for: 17 -> 16; matrix products, arithmetic and copies ran while one was open for 21% -> 23% of each run, Pallas kernels for 9% -> 10%
where the time goes in v3:
time: 285 us; the launch traced here: 282 us
  waiting for transfers between devices  139 us (49%)
  matrix products  67.6 us (24%)
  starting transfers between devices  32.1 us (11%)
  Pallas kernels  27.6 us (10%)
  other arithmetic  9.93 us (3%)
  local copies, waits for them, and re-layouts  3.19 us (1%)
    dot_general x12, matrix products, dot(): lax.dot_general(a, b, ((dims[0], dims[1]), ((), ())), precision=precision...  67.6 us
    ppermute x3, waiting for transfers between devices, per_device(): lax.ppermute(held, 'row', ring_of(n_row))  57 us
    pallas_call x1, Pallas kernels, inverse_factor(): pl.pallas_call(inverse_kernel, out_shape=jax.ShapeDtypeStruct((n, n), F32...  27.6 us
    ppermute x5, waiting for transfers between devices, all_sum(): got = lax.ppermute(held, axis, pairs)  27 us
    ppermute x1, waiting for transfers between devices, per_device(): sketch = lax.ppermute(sketch.astype(BF16), 'col', ring_of(n_col))  12.5 us
    ppermute x3, waiting for transfers between devices, per_device(): lax.ppermute(away.astype(BF16), 'row', pair_of(n_row)).astype(F32)  12 us
    ppermute x1, waiting for transfers between devices, per_device(): lax.ppermute(held, 'col', ring_of(n_col))  11.7 us
    ppermute x5, waiting for transfers between devices, all_sum(): got = lax.ppermute(rows_of(held, (1 - mine) * half, half), axis, pairs)  9.96 us
  transfers between devices with their start and end apart: 31, of which 16 were waited for; matrix products, arithmetic and copies ran while one was open for 23% of the time, Pallas kernels for 10%

profile of v3, /device:TPU:0, one launch (start us, length us, event | category | flops | bytes accessed | tf_op | source)
XLA Modules:
  0.0 281.5 jit_solution(14185782024402433410)
XLA Ops:
  0.6 3.1 %collective-permute-start.1 = (bf16[1024,512]{1,0:T(8,128)(2,1)}, bf16[1024,512]{1,0:T(8,128)(2,1)S(1)}, u32[]{:S(2)}, u32[]{:S(2)}) collective-permute-start(bf16[1024,512]{1,0:T(8,128)(2,1)} %param.3), channel_id=1, source_target_pairs={{0,8},{4,12},{8,16},{12,20},{16,24},{20,28},{24,0},{28,4},{1,9},{5... | collective-permute-start | bytes 3145736 | tf_op jit(solution)/shard_map/ppermute | solution.py:131
  5.2 23.9 %collective-permute-done.1 = bf16[1024,512]{1,0:T(8,128)(2,1)S(1)} collective-permute-done((bf16[1024,512]{1,0:T(8,128)(2,1)}, bf16[1024,512]{1,0:T(8,128)(2,1)S(1)}, u32[]{:S(2)}, u32[]{:S(2)}) %collective-permute-start.1) | collective-permute-done | bytes 1048608 | tf_op jit(solution)/shard_map/ppermute | solution.py:131
  32.0 6.9 %fusion.12 = f32[2048,512]{1,0:T(8,128)S(1)} fusion(bf16[2048,8192]{1,0:T(8,128)(2,1)} %param.2, s32[]{:T(128)S(6)} %select_n.276, bf16[1024,512]{1,0:T(8,128)(2,1)S(1)} %get-tuple-element.13, bf16[1024,512]{1,0:T(8,128)(2,1)S(1)} %get-tuple-element.12), kind=kOutput, calls=%fused_computation.12 | convolution fusion | flops 4299161600 | bytes 14680068 | tf_op jit(solution)/shard_map/dot_general | solution.py:14
  38.9 16.4 %collective-permute-done.3 = bf16[1024,512]{1,0:T(8,128)(2,1)S(1)} collective-permute-done((bf16[1024,512]{1,0:T(8,128)(2,1)S(1)}, bf16[1024,512]{1,0:T(8,128)(2,1)S(1)}, u32[]{:S(2)}, u32[]{:S(2)}) %collective-permute-start.3) | collective-permute-done | bytes 1048608 | tf_op jit(solution)/shard_map/ppermute | solution.py:131
  56.8 6.9 %fusion.8 = f32[2048,512]{1,0:T(8,128)S(1)} fusion(bf16[2048,8192]{1,0:T(8,128)(2,1)} %param.2, s32[]{:T(128)S(6)} %select_n.282, bf16[1024,512]{1,0:T(8,128)(2,1)S(1)} %get-tuple-element.11, bf16[1024,512]{1,0:T(8,128)(2,1)S(1)} %get-tuple-element.10), kind=kOutput, calls=%fused_computation.8 | convolution fusion | flops 4299161600 | bytes 14680068 | tf_op jit(solution)/shard_map/dot_general | solution.py:14
  63.7 16.8 %collective-permute-done.5 = bf16[1024,512]{1,0:T(8,128)(2,1)S(1)} collective-permute-done((bf16[1024,512]{1,0:T(8,128)(2,1)S(1)}, bf16[1024,512]{1,0:T(8,128)(2,1)S(1)}, u32[]{:S(2)}, u32[]{:S(2)}) %collective-permute-start.5) | collective-permute-done | bytes 1048608 | tf_op jit(solution)/shard_map/ppermute | solution.py:131
  82.0 6.9 %fusion.4 = f32[2048,512]{1,0:T(8,128)S(1)} fusion(bf16[2048,8192]{1,0:T(8,128)(2,1)} %param.2, s32[]{:T(128)S(6)} %select_n.286, bf16[1024,512]{1,0:T(8,128)(2,1)S(1)} %get-tuple-element.15, bf16[1024,512]{1,0:T(8,128)(2,1)S(1)} %get-tuple-element.14), kind=kOutput, calls=%fused_computation.4 | convolution fusion | flops 4299161600 | bytes 14680068 | tf_op jit(solution)/shard_map/dot_general | solution.py:14
  88.9 5.1 %add_add_fusion = f32[2048,512]{1,0:T(8,128)S(1)} fusion(f32[2048,512]{1,0:T(8,128)S(1)} %fusion.4, f32[2048,512]{1,0:T(8,128)S(1)} %fusion.12, f32[2048,512]{1,0:T(8,128)S(1)} %fusion.8, bf16[1024,512]{1,0:T(8,128)(2,1)S(1)} %collective-permute-done.5, bf16[2048,8192]{1,0:T(8,128)(2,1)} %param.2, s32[]{:T(128)S(6)} %select_n.290), kind=kOutput, calls=%fused_computation.18 | convolution fusion | flops 2150629376 | bytes 22020100 | tf_op jit(solution)/shard_map/dot_general | solution.py:14
  94.5 4.6 %fusion.14 = f32[2048,512]{1,0:T(8,128)S(1)} fusion(bf16[1024,512]{1,0:T(8,128)(2,1)S(1)} %pad_maximum_fusion, bf16[2048,8192]{1,0:T(8,128)(2,1)} %param.2, s32[]{:T(128)S(6)} %select_n.291), kind=kOutput, calls=%fused_computation.14 | convolution fusion | flops 2147483648 | bytes 9437188 | tf_op jit(solution)/shard_map/dot_general | solution.py:14
  100.1 2.0 copy-done
  102.4 4.2 %collective-permute-done.8 = f32[2,512,512]{2,1,0:T(8,128)} collective-permute-done((f32[2,512,512]{2,1,0:T(8,128)S(1)}, f32[2,512,512]{2,1,0:T(8,128)}, u32[]{:S(2)}, u32[]{:S(2)}) %collective-permute-start.8) | collective-permute-done | bytes 2097184 | tf_op jit(solution)/shard_map/ppermute | solution.py:154
  106.6 2.7 bitcast_add_fusion
  111.0 12.5 %collective-permute-done.9 = bf16[512,512]{1,0:T(8,128)(2,1)S(1)} collective-permute-done((bf16[512,512]{1,0:T(8,128)(2,1)S(1)}, bf16[512,512]{1,0:T(8,128)(2,1)S(1)}, u32[]{:S(2)}, u32[]{:S(2)}) %collective-permute-start.9) | collective-permute-done | bytes 524320 | tf_op jit(solution)/shard_map/ppermute | solution.py:161
  125.2 11.7 %collective-permute-done.11 = bf16[512,512]{1,0:T(8,128)(2,1)} collective-permute-done((bf16[512,512]{1,0:T(8,128)(2,1)S(1)}, bf16[512,512]{1,0:T(8,128)(2,1)}, u32[]{:S(2)}, u32[]{:S(2)}) %collective-permute-start.11) | collective-permute-done | bytes 524320 | tf_op jit(solution)/shard_map/ppermute | solution.py:167
  136.9 1.9 fusion.42
  142.1 7.1 %fusion.6 = f32[2048,512]{1,0:T(8,128)S(1)} fusion(bf16[2048,512]{1,0:T(8,128)(2,1)S(1)} %bitcast.40, bf16[2048,8192]{1,0:T(8,128)(2,1)} %param.2, s32[]{:T(128)S(6)} %select_n.282), kind=kOutput, calls=%fused_computation.6 | convolution fusion | flops 4294967296 | bytes 14680068 | tf_op jit(solution)/shard_map/dot_general | solution.py:14
  149.2 6.9 %fusion = f32[2048,512]{1,0:T(8,128)S(1)} fusion(bf16[2048,512]{1,0:T(8,128)(2,1)S(1)} %bitcast.41, bf16[2048,8192]{1,0:T(8,128)(2,1)} %param.2, s32[]{:T(128)S(6)} %select_n.341), kind=kOutput, calls=%fused_computation | convolution fusion | flops 4294967296 | bytes 14680068 | tf_op jit(solution)/shard_map/dot_general | solution.py:14
  158.7 6.9 %fusion.2 = f32[2048,512]{1,0:T(8,128)S(1)} fusion(bf16[2048,512]{1,0:T(8,128)(2,1)S(1)} %bitcast.42, bf16[2048,8192]{1,0:T(8,128)(2,1)} %param.2, s32[]{:T(128)S(6)} %select_n.339), kind=kOutput, calls=%fused_computation.2 | convolution fusion | flops 4294967296 | bytes 14680068 | tf_op jit(solution)/shard_map/dot_general | solution.py:14
  168.4 5.7 %collective-permute-done.15 = f32[64,512]{1,0:T(8,128)S(1)} collective-permute-done((f32[64,512]{1,0:T(8,128)S(1)}, f32[64,512]{1,0:T(8,128)S(1)}, u32[]{:S(2)}, u32[]{:S(2)}) %collective-permute-start.15) | collective-permute-done | bytes 131104 | tf_op jit(solution)/shard_map/ppermute | solution.py:39
  174.2 3.3 %collective-permute-start.16 = (f32[32,512]{1,0:T(8,128)S(1)}, f32[32,512]{1,0:T(8,128)S(1)}, u32[]{:S(2)}, u32[]{:S(2)}) collective-permute-start(f32[32,512]{1,0:T(8,128)S(1)} %constant_dynamic-slice_fusion.1), channel_id=1, source_target_pairs={{0,8},{4,12},{8,0},{12,4},{16,24},{20,28},{24,16},{28,20},{1,9},{5... | collective-permute-start | bytes 196616 | tf_op jit(solution)/shard_map/ppermute | solution.py:39
  177.6 2.2 collective-permute-done.16
  179.8 3.1 %collective-permute-start.17 = (f32[16,512]{1,0:T(8,128)S(1)}, f32[16,512]{1,0:T(8,128)S(1)}, u32[]{:S(2)}, u32[]{:S(2)}) collective-permute-start(f32[16,512]{1,0:T(8,128)S(1)} %constant_dynamic-slice_fusion), channel_id=1, source_target_pairs={{0,16},{4,20},{8,24},{12,28},{16,0},{20,4},{24,8},{28,12},{1,17},{... | collective-permute-start | bytes 98312 | tf_op jit(solution)/shard_map/ppermute | solution.py:39
  184.8 3.2 %collective-permute-start.18 = (f32[16,512]{1,0:T(8,128)S(1)}, f32[16,512]{1,0:T(8,128)S(1)}, u32[]{:S(2)}, u32[]{:S(2)}) collective-permute-start(f32[16,512]{1,0:T(8,128)S(1)} %dynamic-slice_add_fusion.6), channel_id=1, source_target_pairs={{0,16},{4,20},{8,24},{12,28},{16,0},{20,4},{24,8},{28,12},{1,17},{... | collective-permute-start | bytes 98312 | tf_op jit(solution)/shard_map/ppermute | solution.py:44
  188.6 16.3 %collective-permute-done.18 = f32[16,512]{1,0:T(8,128)S(1)} collective-permute-done((f32[16,512]{1,0:T(8,128)S(1)}, f32[16,512]{1,0:T(8,128)S(1)}, u32[]{:S(2)}, u32[]{:S(2)}) %collective-permute-start.18) | collective-permute-done | bytes 32800 | tf_op jit(solution)/shard_map/ppermute | solution.py:44
  205.2 6.4 %collective-permute-done.19 = f32[32,512]{1,0:T(8,128)S(1)} collective-permute-done((f32[32,512]{1,0:T(8,128)S(1)}, f32[32,512]{1,0:T(8,128)S(1)}, u32[]{:S(2)}, u32[]{:S(2)}) %collective-permute-start.19) | collective-permute-done | bytes 65568 | tf_op jit(solution)/shard_map/ppermute | solution.py:44
  213.8 4.3 %collective-permute-done.20 = f32[64,512]{1,0:T(8,128)S(1)} collective-permute-done((f32[64,512]{1,0:T(8,128)S(1)}, f32[64,512]{1,0:T(8,128)S(1)}, u32[]{:S(2)}, u32[]{:S(2)}) %collective-permute-start.20) | collective-permute-done | bytes 131104 | tf_op jit(solution)/shard_map/ppermute | solution.py:44
  219.7 6.9 %fusion.10 = f32[2048,512]{1,0:T(8,128)S(1)} fusion(bf16[2048,512]{1,0:T(8,128)(2,1)S(1)} %bitcast.43, bf16[2048,8192]{1,0:T(8,128)(2,1)} %param.2, s32[]{:T(128)S(6)} %select_n.276), kind=kOutput, calls=%fused_computation.10 | convolution fusion | flops 4294967296 | bytes 14680068 | tf_op jit(solution)/shard_map/dot_general | solution.py:14
  228.6 12.0 %collective-permute-done.25 = bf16[1024,512]{1,0:T(8,128)(2,1)S(1)} collective-permute-done((bf16[1024,512]{1,0:T(8,128)(2,1)S(1)}, bf16[1024,512]{1,0:T(8,128)(2,1)S(1)}, u32[]{:S(2)}, u32[]{:S(2)}) %collective-permute-start.25) | collective-permute-done | bytes 1048608 | tf_op jit(solution)/shard_map/ppermute | solution.py:203
  241.3 27.6 %shard_map.41 = f32[512,512]{1,0:T(8,128)S(1)} custom-call(f32[512,512]{1,0:T(8,128)S(1)} %maximum_multiply_fusion.gram_ref), custom_call_target="tpu_custom_call" | custom-call | flops 20000000000 | bytes 2097152 | tf_op jit(solution)/shard_map/pallas_call | solution.py:103
  269.0 2.7 convolution_convert_fusion
  271.7 4.7 %collective-permute-done.28 = bf16[1024,512]{1,0:T(8,128)(2,1)S(1)} collective-permute-done((bf16[1024,512]{1,0:T(8,128)(2,1)S(1)}, bf16[1024,512]{1,0:T(8,128)(2,1)S(1)}, u32[]{:S(2)}, u32[]{:S(2)}) %collective-permute-start.28) | collective-permute-done | bytes 1048608 | tf_op jit(solution)/shard_map/ppermute | solution.py:212
  276.4 4.7 %multiply_convert_fusion = bf16[1024,512]{1,0:T(8,128)(2,1)} fusion(f32[512,512]{1,0:T(8,128)S(1)} %shard_map.41, bf16[1024,512]{1,0:T(8,128)(2,1)S(1)} %collective-permute-done.30, bf16[1024,512]{1,0:T(8,128)(2,1)S(1)} %collective-permute-done.28, bf16[1024,512]{1,0:T(8,128)(2,1)S(1)} %collective-permute-done.23, f32[2048,512]{1,0:T(8,128)S(1)} %fusion.10, ...), kind=kOutput, calls=%fused_computation.29 | convolution fusion | flops 3225419776 | bytes 7340036 | tf_op jit(solution)/shard_map/dot_general | solution.py:14
  (93 shorter events, 30.3 us)
Async XLA Ops:
  0.6 28.5 %collective-permute-start.1 = (bf16[1024,512]{1,0:T(8,128)(2,1)}, bf16[1024,512]{1,0:T(8,128)(2,1)S(1)}, u32[]{:S(2)}, u32[]{:S(2)}) collective-permute-start(bf16[1024,512]{1,0:T(8,128)(2,1)} %param.3), channel_id=1, source_target_pairs={{0,8},{4,12},{8,16},{12,20},{16,24},{20,28},{24,0},{28,4},{1,9},{5... | collective-permute-start | bytes 3145736 | tf_op jit(solution)/shard_map/ppermute | solution.py:131
  3.7 26.9 %collective-permute-start = (bf16[1024,512]{1,0:T(8,128)(2,1)}, bf16[1024,512]{1,0:T(8,128)(2,1)S(1)}, u32[]{:S(2)}, u32[]{:S(2)}) collective-permute-start(bf16[1024,512]{1,0:T(8,128)(2,1)} %param.3), channel_id=1, source_target_pairs={{0,4},{4,0},{8,12},{12,8},{16,20},{20,16},{24,28},{28,24},{1,5},{5... | collective-permute-start | bytes 3145736 | tf_op jit(solution)/shard_map/ppermute | solution.py:130
  29.1 26.1 %collective-permute-start.3 = (bf16[1024,512]{1,0:T(8,128)(2,1)S(1)}, bf16[1024,512]{1,0:T(8,128)(2,1)S(1)}, u32[]{:S(2)}, u32[]{:S(2)}) collective-permute-start(bf16[1024,512]{1,0:T(8,128)(2,1)S(1)} %collective-permute-done.1), channel_id=1, source_target_pairs={{0,8},{4,12},{8,16},{12,20},{16,24},{20,28},{24,0},{28,4},{1,9},{5... | collective-permute-start | bytes 3145736 | tf_op jit(solution)/shard_map/ppermute | solution.py:131
  29.1 27.4 %collective-permute-start.2 = (bf16[1024,512]{1,0:T(8,128)(2,1)S(1)}, bf16[1024,512]{1,0:T(8,128)(2,1)S(1)}, u32[]{:S(2)}, u32[]{:S(2)}) collective-permute-start(bf16[1024,512]{1,0:T(8,128)(2,1)S(1)} %collective-permute-done.1), channel_id=1, source_target_pairs={{0,4},{4,0},{8,12},{12,8},{16,20},{20,16},{24,28},{28,24},{1,5},{5... | collective-permute-start | bytes 3145736 | tf_op jit(solution)/shard_map/ppermute | solution.py:130
  55.2 25.2 %collective-permute-start.5 = (bf16[1024,512]{1,0:T(8,128)(2,1)S(1)}, bf16[1024,512]{1,0:T(8,128)(2,1)S(1)}, u32[]{:S(2)}, u32[]{:S(2)}) collective-permute-start(bf16[1024,512]{1,0:T(8,128)(2,1)S(1)} %collective-permute-done.3), channel_id=1, source_target_pairs={{0,8},{4,12},{8,16},{12,20},{16,24},{20,28},{24,0},{28,4},{1,9},{5... | collective-permute-start | bytes 3145736 | tf_op jit(solution)/shard_map/ppermute | solution.py:131
  55.2 26.4 %collective-permute-start.4 = (bf16[1024,512]{1,0:T(8,128)(2,1)S(1)}, bf16[1024,512]{1,0:T(8,128)(2,1)S(1)}, u32[]{:S(2)}, u32[]{:S(2)}) collective-permute-start(bf16[1024,512]{1,0:T(8,128)(2,1)S(1)} %collective-permute-done.3), channel_id=1, source_target_pairs={{0,4},{4,0},{8,12},{12,8},{16,20},{20,16},{24,28},{28,24},{1,5},{5... | collective-permute-start | bytes 3145736 | tf_op jit(solution)/shard_map/ppermute | solution.py:130
  80.5 13.5 %collective-permute-start.6 = (bf16[512,512]{1,0:T(8,128)(2,1)S(1)}, bf16[512,512]{1,0:T(8,128)(2,1)S(1)}, u32[]{:S(2)}, u32[]{:S(2)}) collective-permute-start(bf16[512,512]{1,0:T(8,128)(2,1)S(1)} %slice.36), channel_id=1, source_target_pairs={{0,4},{4,0},{8,12},{12,8},{16,20},{20,16},{24,28},{28,24},{1,5},{5... | collective-permute-start | bytes 1572872 | tf_op jit(solution)/shard_map/ppermute | solution.py:126
  81.6 12.8 %collective-permute-start.7 = (bf16[512,512]{1,0:T(8,128)(2,1)S(1)}, bf16[512,512]{1,0:T(8,128)(2,1)S(1)}, u32[]{:S(2)}, u32[]{:S(2)}) collective-permute-start(bf16[512,512]{1,0:T(8,128)(2,1)S(1)} %slice.37), channel_id=1, source_target_pairs={{0,8},{4,12},{8,16},{12,20},{16,24},{20,28},{24,0},{28,4},{1,9},{5... | collective-permute-start | bytes 1572872 | tf_op jit(solution)/shard_map/ppermute | solution.py:127
  100.1 2.0 copy-start
  102.3 4.4 %collective-permute-start.8 = (f32[2,512,512]{2,1,0:T(8,128)S(1)}, f32[2,512,512]{2,1,0:T(8,128)}, u32[]{:S(2)}, u32[]{:S(2)}) collective-permute-start(f32[2,512,512]{2,1,0:T(8,128)S(1)} %dynamic-slice_bitcast_fusion), channel_id=1, source_target_pairs={{0,1},{1,0},{2,3},{3,2},{4,5},{5,4},{6,7},{7,6},{8,9},{9,8},{10,11... | collective-permute-start | bytes 6291464 | tf_op jit(solution)/shard_map/ppermute | solution.py:154
  109.4 14.0 %collective-permute-start.9 = (bf16[512,512]{1,0:T(8,128)(2,1)S(1)}, bf16[512,512]{1,0:T(8,128)(2,1)S(1)}, u32[]{:S(2)}, u32[]{:S(2)}) collective-permute-start(bf16[512,512]{1,0:T(8,128)(2,1)S(1)} %fusion.41), channel_id=1, source_target_pairs={{0,2},{1,3},{2,0},{3,1},{4,6},{5,7},{6,4},{7,5},{8,10},{9,11},{10,... | collective-permute-start | bytes 1572872 | tf_op jit(solution)/shard_map/ppermute | solution.py:161
  123.6 13.3 %collective-permute-start.11 = (bf16[512,512]{1,0:T(8,128)(2,1)S(1)}, bf16[512,512]{1,0:T(8,128)(2,1)}, u32[]{:S(2)}, u32[]{:S(2)}) collective-permute-start(bf16[512,512]{1,0:T(8,128)(2,1)S(1)} %fusion.43), channel_id=1, source_target_pairs={{0,2},{1,3},{2,0},{3,1},{4,6},{5,7},{6,4},{7,5},{8,10},{9,11},{10,... | collective-permute-start | bytes 1572872 | tf_op jit(solution)/shard_map/ppermute | solution.py:167
  125.2 13.7 %collective-permute-start.10 = (bf16[512,512]{1,0:T(8,128)(2,1)S(1)}, bf16[512,512]{1,0:T(8,128)(2,1)}, u32[]{:S(2)}, u32[]{:S(2)}) collective-permute-start(bf16[512,512]{1,0:T(8,128)(2,1)S(1)} %fusion.43), channel_id=1, source_target_pairs={{0,1},{1,0},{2,3},{3,2},{4,5},{5,4},{6,7},{7,6},{8,9},{9,8},{10,11... | collective-permute-start | bytes 1572872 | tf_op jit(solution)/shard_map/ppermute | solution.py:166
  136.9 3.3 %collective-permute-start.12 = (bf16[512,512]{1,0:T(8,128)(2,1)}, bf16[512,512]{1,0:T(8,128)(2,1)S(1)}, u32[]{:S(2)}, u32[]{:S(2)}) collective-permute-start(bf16[512,512]{1,0:T(8,128)(2,1)} %collective-permute-done.11), channel_id=1, source_target_pairs={{0,1},{1,0},{2,3},{3,2},{4,5},{5,4},{6,7},{7,6},{8,9},{9,8},{10,11... | collective-permute-start | bytes 1572872 | tf_op jit(solution)/shard_map/ppermute | solution.py:166
  141.5 16.3 %collective-permute-start.13 = (f32[256,512]{1,0:T(8,128)S(1)}, f32[256,512]{1,0:T(8,128)S(1)}, u32[]{:S(2)}, u32[]{:S(2)}) collective-permute-start(f32[256,512]{1,0:T(8,128)S(1)} %constant_dynamic-slice_fusion.4), channel_id=1, source_target_pairs={{0,1},{1,0},{2,3},{3,2},{4,5},{5,4},{6,7},{7,6},{8,9},{9,8},{10,11... | collective-permute-start | bytes 1572872 | tf_op jit(solution)/shard_map/ppermute | solution.py:39
  156.4 48.6 %collective-permute-start.24 = (bf16[512,512]{1,0:T(8,128)(2,1)S(1)}, bf16[512,512]{1,0:T(8,128)(2,1)S(1)}, u32[]{:S(2)}, u32[]{:S(2)}) collective-permute-start(bf16[512,512]{1,0:T(8,128)(2,1)S(1)} %get-tuple-element.16), channel_id=1, source_target_pairs={{0,8},{4,12},{8,16},{12,20},{16,24},{20,28},{24,0},{28,4},{1,9},{5... | collective-permute-start | bytes 1572872 | tf_op jit(solution)/shard_map/ppermute | solution.py:197
  156.5 26.4 %collective-permute-start.26 = (bf16[512,512]{1,0:T(8,128)(2,1)S(1)}, bf16[512,512]{1,0:T(8,128)(2,1)S(1)}, u32[]{:S(2)}, u32[]{:S(2)}) collective-permute-start(bf16[512,512]{1,0:T(8,128)(2,1)S(1)} %get-tuple-element.17), channel_id=1, source_target_pairs={{0,4},{4,0},{8,12},{12,8},{16,20},{20,16},{24,28},{28,24},{1,5},{5... | collective-permute-start | bytes 1572872 | tf_op jit(solution)/shard_map/ppermute | solution.py:198
  157.9 8.0 %collective-permute-start.14 = (f32[128,512]{1,0:T(8,128)S(1)}, f32[128,512]{1,0:T(8,128)S(1)}, u32[]{:S(2)}, u32[]{:S(2)}) collective-permute-start(f32[128,512]{1,0:T(8,128)S(1)} %constant_dynamic-slice_fusion.3), channel_id=1, source_target_pairs={{0,2},{1,3},{2,0},{3,1},{4,6},{5,7},{6,4},{7,5},{8,10},{9,11},{10,... | collective-permute-start | bytes 786440 | tf_op jit(solution)/shard_map/ppermute | solution.py:39
  166.0 8.1 %collective-permute-start.15 = (f32[64,512]{1,0:T(8,128)S(1)}, f32[64,512]{1,0:T(8,128)S(1)}, u32[]{:S(2)}, u32[]{:S(2)}) collective-permute-start(f32[64,512]{1,0:T(8,128)S(1)} %constant_dynamic-slice_fusion.2), channel_id=1, source_target_pairs={{0,4},{4,0},{8,12},{12,8},{16,20},{20,16},{24,28},{28,24},{1,5},{5... | collective-permute-start | bytes 393224 | tf_op jit(solution)/shard_map/ppermute | solution.py:39
  167.5 60.4 %collective-permute-start.29 = (bf16[1024,512]{1,0:T(8,128)(2,1)S(1)}, bf16[1024,512]{1,0:T(8,128)(2,1)S(1)}, u32[]{:S(2)}, u32[]{:S(2)}) collective-permute-start(bf16[1024,512]{1,0:T(8,128)(2,1)S(1)} %dynamic-slice_convert_fusion), channel_id=1, source_target_pairs={{0,4},{4,0},{8,12},{12,8},{16,20},{20,16},{24,28},{28,24},{1,5},{5... | collective-permute-start | bytes 3145736 | tf_op jit(solution)/shard_map/ppermute | solution.py:203
  174.2 5.6 %collective-permute-start.16 = (f32[32,512]{1,0:T(8,128)S(1)}, f32[32,512]{1,0:T(8,128)S(1)}, u32[]{:S(2)}, u32[]{:S(2)}) collective-permute-start(f32[32,512]{1,0:T(8,128)S(1)} %constant_dynamic-slice_fusion.1), channel_id=1, source_target_pairs={{0,8},{4,12},{8,0},{12,4},{16,24},{20,28},{24,16},{28,20},{1,9},{5... | collective-permute-start | bytes 196616 | tf_op jit(solution)/shard_map/ppermute | solution.py:39
  179.8 5.0 %collective-permute-start.17 = (f32[16,512]{1,0:T(8,128)S(1)}, f32[16,512]{1,0:T(8,128)S(1)}, u32[]{:S(2)}, u32[]{:S(2)}) collective-permute-start(f32[16,512]{1,0:T(8,128)S(1)} %constant_dynamic-slice_fusion), channel_id=1, source_target_pairs={{0,16},{4,20},{8,24},{12,28},{16,0},{20,4},{24,8},{28,12},{1,17},{... | collective-permute-start | bytes 98312 | tf_op jit(solution)/shard_map/ppermute | solution.py:39
  184.8 20.1 %collective-permute-start.18 = (f32[16,512]{1,0:T(8,128)S(1)}, f32[16,512]{1,0:T(8,128)S(1)}, u32[]{:S(2)}, u32[]{:S(2)}) collective-permute-start(f32[16,512]{1,0:T(8,128)S(1)} %dynamic-slice_add_fusion.6), channel_id=1, source_target_pairs={{0,16},{4,20},{8,24},{12,28},{16,0},{20,4},{24,8},{28,12},{1,17},{... | collective-permute-start | bytes 98312 | tf_op jit(solution)/shard_map/ppermute | solution.py:44
  188.1 40.5 %collective-permute-start.27 = (bf16[1024,512]{1,0:T(8,128)(2,1)S(1)}, bf16[1024,512]{1,0:T(8,128)(2,1)S(1)}, u32[]{:S(2)}, u32[]{:S(2)}) collective-permute-start(bf16[1024,512]{1,0:T(8,128)(2,1)S(1)} %pad_maximum_fusion.2), channel_id=1, source_target_pairs={{0,8},{4,12},{8,16},{12,20},{16,24},{20,28},{24,0},{28,4},{1,9},{5... | collective-permute-start | bytes 3145736 | tf_op jit(solution)/shard_map/ppermute | solution.py:212
  204.9 6.6 %collective-permute-start.19 = (f32[32,512]{1,0:T(8,128)S(1)}, f32[32,512]{1,0:T(8,128)S(1)}, u32[]{:S(2)}, u32[]{:S(2)}) collective-permute-start(f32[32,512]{1,0:T(8,128)S(1)} %pad_maximum_fusion.6), channel_id=1, source_target_pairs={{0,8},{4,12},{8,0},{12,4},{16,24},{20,28},{24,16},{28,20},{1,9},{5... | collective-permute-start | bytes 196616 | tf_op jit(solution)/shard_map/ppermute | solution.py:44
  211.6 6.5 %collective-permute-start.20 = (f32[64,512]{1,0:T(8,128)S(1)}, f32[64,512]{1,0:T(8,128)S(1)}, u32[]{:S(2)}, u32[]{:S(2)}) collective-permute-start(f32[64,512]{1,0:T(8,128)S(1)} %pad_maximum_fusion.5), channel_id=1, source_target_pairs={{0,4},{4,0},{8,12},{12,8},{16,20},{20,16},{24,28},{28,24},{1,5},{5... | collective-permute-start | bytes 393224 | tf_op jit(solution)/shard_map/ppermute | solution.py:44
  212.9 27.7 %collective-permute-start.25 = (bf16[1024,512]{1,0:T(8,128)(2,1)S(1)}, bf16[1024,512]{1,0:T(8,128)(2,1)S(1)}, u32[]{:S(2)}, u32[]{:S(2)}) collective-permute-start(bf16[1024,512]{1,0:T(8,128)(2,1)S(1)} %pad_maximum_fusion.1), channel_id=1, source_target_pairs={{0,4},{4,0},{8,12},{12,8},{16,20},{20,16},{24,28},{28,24},{1,5},{5... | collective-permute-start | bytes 3145736 | tf_op jit(solution)/shard_map/ppermute | solution.py:203
  218.2 9.6 %collective-permute-start.21 = (f32[128,512]{1,0:T(8,128)S(1)}, f32[128,512]{1,0:T(8,128)S(1)}, u32[]{:S(2)}, u32[]{:S(2)}) collective-permute-start(f32[128,512]{1,0:T(8,128)S(1)} %pad_maximum_fusion.4), channel_id=1, source_target_pairs={{0,2},{1,3},{2,0},{3,1},{4,6},{5,7},{6,4},{7,5},{8,10},{9,11},{10,... | collective-permute-start | bytes 786440 | tf_op jit(solution)/shard_map/ppermute | solution.py:44
  226.8 44.9 %collective-permute-start.23 = (bf16[1024,512]{1,0:T(8,128)(2,1)S(1)}, bf16[1024,512]{1,0:T(8,128)(2,1)S(1)}, u32[]{:S(2)}, u32[]{:S(2)}) collective-permute-start(bf16[1024,512]{1,0:T(8,128)(2,1)S(1)} %dynamic-slice_convert_fusion.2), channel_id=1, source_target_pairs={{0,4},{4,0},{8,12},{12,8},{16,20},{20,16},{24,28},{28,24},{1,5},{5... | collective-permute-start | bytes 3145736 | tf_op jit(solution)/shard_map/ppermute | solution.py:203
  227.8 13.3 %collective-permute-start.22 = (f32[256,512]{1,0:T(8,128)S(1)}, f32[256,512]{1,0:T(8,128)S(1)}, u32[]{:S(2)}, u32[]{:S(2)}) collective-permute-start(f32[256,512]{1,0:T(8,128)S(1)} %pad_maximum_fusion.3), channel_id=1, source_target_pairs={{0,1},{1,0},{2,3},{3,2},{4,5},{5,4},{6,7},{7,6},{8,9},{9,8},{10,11... | collective-permute-start | bytes 1572872 | tf_op jit(solution)/shard_map/ppermute | solution.py:44
  228.3 43.4 %collective-permute-start.30 = (bf16[1024,512]{1,0:T(8,128)(2,1)S(1)}, bf16[1024,512]{1,0:T(8,128)(2,1)S(1)}, u32[]{:S(2)}, u32[]{:S(2)}) collective-permute-start(bf16[1024,512]{1,0:T(8,128)(2,1)S(1)} %add_convert_fusion), channel_id=1, source_target_pairs={{8,0},{12,4},{16,8},{20,12},{24,16},{28,20},{0,24},{4,28},{9,1},{1... | collective-permute-start | bytes 3145736 | tf_op jit(solution)/shard_map/ppermute | solution.py:212
  241.0 35.3 %collective-permute-start.28 = (bf16[1024,512]{1,0:T(8,128)(2,1)S(1)}, bf16[1024,512]{1,0:T(8,128)(2,1)S(1)}, u32[]{:S(2)}, u32[]{:S(2)}) collective-permute-start(bf16[1024,512]{1,0:T(8,128)(2,1)S(1)} %add_convert_fusion.1), channel_id=1, source_target_pairs={{0,8},{4,12},{8,16},{12,20},{16,24},{20,28},{24,0},{28,4},{1,9},{5... | collective-permute-start | bytes 3145736 | tf_op jit(solution)/shard_map/ppermute | solution.py:212

commit v4 on v3

--- a/solution.py
+++ b/solution.py
@@ -1,3 +1,5 @@
+import functools
+
 import jax
 import jax.numpy as jnp
 from jax import lax
@@ -27,25 +29,80 @@
     return lax.dynamic_slice_in_dim(x, start, count, 0)
 
 
-def all_sum(gram, sizes):
-    steps = []
-    held = gram
-    for axis, n in sizes:
-        bit = 1
-        while bit < n:
-            half = held.shape[0] // 2
-            mine = (lax.axis_index(axis) // bit) % 2
-            pairs = [(i, i ^ bit) for i in range(n)]
-            got = lax.ppermute(rows_of(held, (1 - mine) * half, half), axis, pairs)
-            held = rows_of(held, mine * half, half) + got
-            steps.append((axis, pairs, mine))
-            bit *= 2
-    for axis, pairs, mine in reversed(steps):
-        got = lax.ppermute(held, axis, pairs)
-        low = jnp.where(mine == 0, held, got)
-        high = jnp.where(mine == 0, got, held)
-        held = jnp.concatenate([low, high], 0)
-    return held
+def other_of(index, bit):
+    return index + bit - 2 * bit * ((index // bit) % 2)
+
+
+def gram_sum_kernel(n_row, n_col, gram_ref, out_ref, land_ref, send_sem, recv_sem):
+    me, col = lax.axis_index("row"), lax.axis_index("col")
+    bits = [1 << i for i in reversed(range(n_col.bit_length() - 1))]
+    mesh_id = pl.DeviceIdType.MESH
+
+    barrier = pltpu.get_barrier_semaphore()
+    for d in range(1, n_row):
+        pl.semaphore_signal(barrier, inc=1, device_id={"row": (me + d) % n_row}, device_id_type=mesh_id)
+    for bit in bits:
+        pl.semaphore_signal(barrier, inc=1, device_id={"col": other_of(col, bit)}, device_id_type=mesh_id)
+    pl.semaphore_wait(barrier, n_row - 1 + len(bits))
+
+    sent = []
+
+    def send(source, target, sem, device):
+        copy = pltpu.make_async_remote_copy(
+            src_ref=source, dst_ref=target, send_sem=send_sem.at[sem], recv_sem=recv_sem.at[sem],
+            device_id=device, device_id_type=mesh_id)
+        copy.start()
+        sent.append(copy)
+        return copy
+
+    first = []
+    for d in range(1, n_row):
+        peer = (me + d) % n_row
+        first.append(send(gram_ref.at[peer], land_ref.at[d - 1], d - 1, {"row": peer}))
+    total = gram_ref[me]
+    for d in range(1, n_row):
+        first[d - 1].wait_recv()
+        total = total + land_ref[d - 1]
+    out_ref[col, me] = total
+    second = []
+    for d in range(1, n_row):
+        peer = (me + d) % n_row
+        second.append(send(out_ref.at[col, me], out_ref.at[col, me], n_row - 2 + d, {"row": peer}))
+    for copy in second:
+        copy.wait_recv()
+    held = [col]
+    sem = 2 * (n_row - 1)
+    for bit in bits:
+        third = []
+        for share in held:
+            third.append(send(out_ref.at[share], out_ref.at[share], sem, {"col": other_of(col, bit)}))
+            sem += 1
+        for copy in third:
+            copy.wait_recv()
+        held = held + [other_of(share, bit) for share in held]
+    for copy in sent:
+        copy.wait_send()
+
+
+def gram_sum(share, n_row, n_col):
+    rows, n = share.shape
+    m = rows // n_row
+    count = 2 * (n_row - 1) + n_col - 1
+    whole = pl.pallas_call(
+        functools.partial(gram_sum_kernel, n_row, n_col),
+        out_shape=jax.ShapeDtypeStruct((n_col, n_row, m, n), F32),
+        in_specs=[pl.BlockSpec(memory_space=pltpu.VMEM)],
+        out_specs=pl.BlockSpec(memory_space=pltpu.VMEM),
+        scratch_shapes=[
+            pltpu.VMEM((n_row - 1, m, n), F32),
+            pltpu.SemaphoreType.DMA((count,)),
+            pltpu.SemaphoreType.DMA((count,)),
+        ],
+        cost_estimate=pl.CostEstimate(flops=20_000_000_000, bytes_accessed=8 * n * n, transcendentals=0),
+        compiler_params=pltpu.CompilerParams(
+            collective_id=0, has_side_effects=True, vmem_limit_bytes=24 * 2**20),
+    )(share.reshape(n_row, m, n))
+    return whole.reshape(n, n)
 
 
 def inverse_kernel(gram_ref, out_ref, work_ref, aug_ref):
@@ -170,15 +227,6 @@
         held = later
     full = full.reshape(n_col * rows, rank)
 
-    gram = dot(sketch, sketch, ((0,), (0,)), HIGH)
-    full, gram = lax.optimization_barrier((full, gram))
-    gram = all_sum(gram, (("col", n_col), ("row", n_row)))
-    inverse = inverse_factor(gram / F32(d))
-
-    def term_of(at):
-        cut = lax.dynamic_slice_in_dim(weight, at * 2 * depth, 2 * depth, 1)
-        return dot(cut, full, ((0,), (0,)))
-
     up_hops = ring // 2
     down_hops = ring - 1 - up_hops
     order = []
@@ -187,10 +235,15 @@
         if step < down_hops:
             order.append(step - down_hops)
     order.append(0)
+    share = rank // n_col
+    gram = dot(lax.dynamic_slice_in_dim(full, col * share, share, 1), full, ((0,), (0,)))
+    gram = gram_sum(gram, n_row, n_col)
+    full, gram = lax.optimization_barrier((full, gram))
     terms = {}
-    early = None
-    for at in order:
-        term = term_of((group + at + ring) % ring)
+
+    def add_term(at, full, early):
+        cut = lax.dynamic_slice_in_dim(weight, (group + at + ring) % ring * 2 * depth, 2 * depth, 1)
+        term = dot(cut, full, ((0,), (0,)))
         near = rows_of(term, side * depth, depth)
         away = rows_of(term, (1 - side) * depth, depth)
         if at == up_hops and at:
@@ -202,18 +255,29 @@
                 away = jnp.concatenate([away[:half], away[half:] + early.astype(F32)], 0)
             near = near + lax.ppermute(away.astype(BF16), "row", pair_of(n_row)).astype(F32)
         terms[at] = near
-
-    def travel(hops, sign, pairs):
-        moving = None
-        for step in range(hops):
-            own = terms[sign * (hops - step)]
-            if moving is not None:
-                own = own + moving.astype(F32)
-            moving = lax.ppermute(own.astype(BF16), "row", pairs)
-        return moving
-
-    up = travel(up_hops, 1, ring_of(n_row))
-    down = travel(down_hops, -1, down_ring)
+        return early
+
+    def hop(own, moving, pairs):
+        if moving is not None:
+            own = own + moving.astype(F32)
+        return lax.ppermute(own.astype(BF16), "row", pairs)
+
+    early = None
+    for at in order[:-1]:
+        early = add_term(at, full, early)
+    up = down = None
+    for step in range(down_hops):
+        own = terms[step - down_hops]
+        if step == 0:
+            own, gram = lax.optimization_barrier((own, gram))
+        down = hop(own, down, down_ring)
+    inverse = inverse_factor(gram / F32(d))
+    for step in range(up_hops):
+        own = terms[up_hops - step]
+        if step + 1 == up_hops:
+            own, inverse = lax.optimization_barrier((own, inverse))
+        up = hop(own, up, ring_of(n_row))
+    add_term(0, full, early)
     factor = terms[0]
     for moved in (up, down):
         if moved is not None:

time: 285 us -> 313 us (1.098)
  Pallas kernels: 27.6 us -> 51.5 us
  waiting for transfers between devices: 139 us -> 150 us
  starting transfers between devices: 32.1 us -> 26 us
    pallas_call x0 -> x1, Pallas kernels: none -> 23.8 us  [gram_sum(): pl.pallas_call(functools.partial(gram_sum_kernel, n_row, n_col), out_shap...]
    ppermute x18 -> x8, waiting for transfers between devices: 53.6 us -> 62.4 us  [the longest x3 29.6 us: hop(): return lax.ppermute(own.astype(BF16), 'row', pairs)]
    ppermute x18 -> x8, starting transfers between devices: 20.2 us -> 14.6 us  [the longest x3 7.89 us: hop(): return lax.ppermute(own.astype(BF16), 'row', pairs)]
  transfers between devices with their start and end apart: 31 -> 21, of which waited for: 16 -> 13; matrix products, arithmetic and copies ran while one was open for 23% -> 13% of each run, Pallas kernels for 10% -> 9%
where the time goes in v4:
time: 313 us; the launch traced here: 312 us
  waiting for transfers between devices  150 us (48%)
  matrix products  67.9 us (22%)
  Pallas kernels  51.5 us (16%)
  starting transfers between devices  26 us (8%)
  other arithmetic  9.9 us (3%)
  local copies, waits for them, and re-layouts  5.47 us (2%)
    dot_general x12, matrix products, dot(): lax.dot_general(a, b, ((dims[0], dims[1]), ((), ())), precision=precision...  67.9 us
    ppermute x3, waiting for transfers between devices, per_device(): lax.ppermute(held, 'row', ring_of(n_row))  58.7 us
    ppermute x3, waiting for transfers between devices, hop(): return lax.ppermute(own.astype(BF16), 'row', pairs)  29.6 us
    pallas_call x1, Pallas kernels, inverse_factor(): pl.pallas_call(inverse_kernel, out_shape=jax.ShapeDtypeStruct((n, n), F32...  27.6 us
    ppermute x3, waiting for transfers between devices, add_term(): lax.ppermute(away.astype(BF16), 'row', pair_of(n_row)).astype(F32)  26.6 us
    pallas_call x1, Pallas kernels, gram_sum(): pl.pallas_call(functools.partial(gram_sum_kernel, n_row, n_col), out_shap...  23.8 us
    ppermute x1, waiting for transfers between devices, per_device(): sketch = lax.ppermute(sketch.astype(BF16), 'col', ring_of(n_col))  12.5 us
    ppermute x1, waiting for transfers between devices, per_device(): lax.ppermute(held, 'col', ring_of(n_col))  11.7 us
  transfers between devices with their start and end apart: 21, of which 13 were waited for; matrix products, arithmetic and copies ran while one was open for 13% of the time, Pallas kernels for 9%

profile of v4, /device:TPU:0, one launch (start us, length us, event | category | flops | bytes accessed | tf_op | source)
XLA Modules:
  0.0 312.3 jit_solution(5797154690381307101)
XLA Ops:
  0.6 3.1 collective-permute-start.1
  5.2 23.9 %collective-permute-done.1 = bf16[1024,512]{1,0:T(8,128)(2,1)S(1)} collective-permute-done((bf16[1024,512]{1,0:T(8,128)(2,1)}, bf16[1024,512]{1,0:T(8,128)(2,1)S(1)}, u32[]{:S(2)}, u32[]{:S(2)}) %collective-permute-start.1) | collective-permute-done | bytes 1048608 | tf_op jit(solution)/shard_map/ppermute | solution.py:188
  32.0 6.9 %fusion.12 = f32[2048,512]{1,0:T(8,128)S(1)} fusion(bf16[2048,8192]{1,0:T(8,128)(2,1)} %param.2, s32[]{:T(128)S(6)} %select_n.166, bf16[1024,512]{1,0:T(8,128)(2,1)S(1)} %get-tuple-element.21, bf16[1024,512]{1,0:T(8,128)(2,1)S(1)} %get-tuple-element.20), kind=kOutput, calls=%fused_computation.12 | convolution fusion | flops 4299161600 | bytes 14680068 | tf_op jit(solution)/shard_map/dot_general | solution.py:16
  38.9 17.3 %collective-permute-done.3 = bf16[1024,512]{1,0:T(8,128)(2,1)S(1)} collective-permute-done((bf16[1024,512]{1,0:T(8,128)(2,1)S(1)}, bf16[1024,512]{1,0:T(8,128)(2,1)S(1)}, u32[]{:S(2)}, u32[]{:S(2)}) %collective-permute-start.3) | collective-permute-done | bytes 1048608 | tf_op jit(solution)/shard_map/ppermute | solution.py:188
  57.3 6.9 %fusion.8 = f32[2048,512]{1,0:T(8,128)S(1)} fusion(bf16[2048,8192]{1,0:T(8,128)(2,1)} %param.2, s32[]{:T(128)S(6)} %select_n.172, bf16[1024,512]{1,0:T(8,128)(2,1)S(1)} %get-tuple-element.19, bf16[1024,512]{1,0:T(8,128)(2,1)S(1)} %get-tuple-element.18), kind=kOutput, calls=%fused_computation.8 | convolution fusion | flops 4299161600 | bytes 14680068 | tf_op jit(solution)/shard_map/dot_general | solution.py:16
  64.2 17.5 %collective-permute-done.5 = bf16[1024,512]{1,0:T(8,128)(2,1)S(1)} collective-permute-done((bf16[1024,512]{1,0:T(8,128)(2,1)S(1)}, bf16[1024,512]{1,0:T(8,128)(2,1)S(1)}, u32[]{:S(2)}, u32[]{:S(2)}) %collective-permute-start.5) | collective-permute-done | bytes 1048608 | tf_op jit(solution)/shard_map/ppermute | solution.py:188
  83.2 6.9 %fusion.4 = f32[2048,512]{1,0:T(8,128)S(1)} fusion(bf16[2048,8192]{1,0:T(8,128)(2,1)} %param.2, s32[]{:T(128)S(6)} %select_n.176, bf16[1024,512]{1,0:T(8,128)(2,1)S(1)} %get-tuple-element.23, bf16[1024,512]{1,0:T(8,128)(2,1)S(1)} %get-tuple-element.22), kind=kOutput, calls=%fused_computation.4 | convolution fusion | flops 4299161600 | bytes 14680068 | tf_op jit(solution)/shard_map/dot_general | solution.py:16
  90.1 5.0 %add_add_fusion = f32[2048,512]{1,0:T(8,128)S(1)} fusion(f32[2048,512]{1,0:T(8,128)S(1)} %fusion.4, f32[2048,512]{1,0:T(8,128)S(1)} %fusion.12, f32[2048,512]{1,0:T(8,128)S(1)} %fusion.8, bf16[1024,512]{1,0:T(8,128)(2,1)S(1)} %collective-permute-done.5, bf16[2048,8192]{1,0:T(8,128)(2,1)} %param.2, s32[]{:T(128)S(6)} %select_n.180), kind=kOutput, calls=%fused_computation.18 | convolution fusion | flops 2150629376 | bytes 22020100 | tf_op jit(solution)/shard_map/dot_general | solution.py:16
  95.3 4.6 %fusion.14 = f32[2048,512]{1,0:T(8,128)S(1)} fusion(bf16[1024,512]{1,0:T(8,128)(2,1)S(1)} %pad_maximum_fusion, bf16[2048,8192]{1,0:T(8,128)(2,1)} %param.2, s32[]{:T(128)S(6)} %select_n.181), kind=kOutput, calls=%fused_computation.14 | convolution fusion | flops 2147483648 | bytes 9437188 | tf_op jit(solution)/shard_map/dot_general | solution.py:16
  100.9 1.9 copy-done
  103.2 4.2 %collective-permute-done.8 = f32[2,512,512]{2,1,0:T(8,128)} collective-permute-done((f32[2,512,512]{2,1,0:T(8,128)S(1)}, f32[2,512,512]{2,1,0:T(8,128)}, u32[]{:S(2)}, u32[]{:S(2)}) %collective-permute-start.8) | collective-permute-done | bytes 2097184 | tf_op jit(solution)/shard_map/ppermute | solution.py:211
  107.4 2.7 bitcast_add_fusion
  111.7 12.5 %collective-permute-done.9 = bf16[512,512]{1,0:T(8,128)(2,1)S(1)} collective-permute-done((bf16[512,512]{1,0:T(8,128)(2,1)S(1)}, bf16[512,512]{1,0:T(8,128)(2,1)S(1)}, u32[]{:S(2)}, u32[]{:S(2)}) %collective-permute-start.9) | collective-permute-done | bytes 524320 | tf_op jit(solution)/shard_map/ppermute | solution.py:218
  125.9 11.7 %collective-permute-done.11 = bf16[512,512]{1,0:T(8,128)(2,1)} collective-permute-done((bf16[512,512]{1,0:T(8,128)(2,1)S(1)}, bf16[512,512]{1,0:T(8,128)(2,1)}, u32[]{:S(2)}, u32[]{:S(2)}) %collective-permute-start.11) | collective-permute-done | bytes 524320 | tf_op jit(solution)/shard_map/ppermute | solution.py:224
  143.7 2.2 fusion.60.gram_ref
  146.0 23.8 %shard_map.41 = f32[4,8,16,512]{3,2,1,0:T(8,128)S(1)} custom-call(f32[8,16,512]{2,1,0:T(8,128)S(1)} %fusion.60.gram_ref), custom_call_target="tpu_custom_call" | custom-call | flops 20000000000 | bytes 2097152 | tf_op jit(solution)/shard_map/pallas_call | solution.py:91
  169.8 6.9 %fusion.6 = f32[2048,512]{1,0:T(8,128)S(1)} fusion(bf16[2048,512]{1,0:T(8,128)(2,1)S(1)} %bitcast.50, bf16[2048,8192]{1,0:T(8,128)(2,1)} %param.2, s32[]{:T(128)S(6)} %select_n.172), kind=kOutput, calls=%fused_computation.6 | convolution fusion | flops 4294967296 | bytes 14680068 | tf_op jit(solution)/shard_map/dot_general | solution.py:16
  176.8 7.2 %fusion.10 = f32[2048,512]{1,0:T(8,128)S(1)} fusion(bf16[2048,512]{1,0:T(8,128)(2,1)S(1)} %bitcast.51, bf16[2048,8192]{1,0:T(8,128)(2,1)} %param.2, s32[]{:T(128)S(6)} %select_n.166), kind=kOutput, calls=%fused_computation.10 | convolution fusion | flops 4294967296 | bytes 14680068 | tf_op jit(solution)/shard_map/dot_general | solution.py:16
  183.9 6.9 %fusion = f32[2048,512]{1,0:T(8,128)S(1)} fusion(bf16[2048,512]{1,0:T(8,128)(2,1)S(1)} %bitcast.52, bf16[2048,8192]{1,0:T(8,128)(2,1)} %param.2, s32[]{:T(128)S(6)} %select_n.203), kind=kOutput, calls=%fused_computation | convolution fusion | flops 4294967296 | bytes 14680068 | tf_op jit(solution)/shard_map/dot_general | solution.py:16
  191.1 2.4 collective-permute-start.17
  195.1 6.9 %fusion.2 = f32[2048,512]{1,0:T(8,128)S(1)} fusion(bf16[2048,512]{1,0:T(8,128)(2,1)S(1)} %bitcast.53, bf16[2048,8192]{1,0:T(8,128)(2,1)} %param.2, s32[]{:T(128)S(6)} %select_n.191), kind=kOutput, calls=%fused_computation.2 | convolution fusion | flops 4294967296 | bytes 14680068 | tf_op jit(solution)/shard_map/dot_general | solution.py:16
  203.5 2.8 collective-permute-done.17
  207.9 3.4 %collective-permute-done.13 = bf16[512,512]{1,0:T(8,128)(2,1)S(1)} collective-permute-done((bf16[512,512]{1,0:T(8,128)(2,1)S(1)}, bf16[512,512]{1,0:T(8,128)(2,1)S(1)}, u32[]{:S(2)}, u32[]{:S(2)}) %collective-permute-start.13) | collective-permute-done | bytes 524320 | tf_op jit(solution)/shard_map/ppermute | solution.py:250
  211.5 1.7 collective-permute-start.14
  213.3 15.4 %collective-permute-done.15 = bf16[1024,512]{1,0:T(8,128)(2,1)S(1)} collective-permute-done((bf16[1024,512]{1,0:T(8,128)(2,1)S(1)}, bf16[1024,512]{1,0:T(8,128)(2,1)S(1)}, u32[]{:S(2)}, u32[]{:S(2)}) %collective-permute-start.15) | collective-permute-done | bytes 1048608 | tf_op jit(solution)/shard_map/ppermute | solution.py:256
  229.2 27.6 %shard_map.42 = f32[512,512]{1,0:T(8,128)S(1)} custom-call(f32[512,512]{1,0:T(8,128)S(1)} %broadcast_multiply_fusion.gram_ref), custom_call_target="tpu_custom_call" | custom-call | flops 20000000000 | bytes 2097152 | tf_op jit(solution)/shard_map/pallas_call | solution.py:160
  256.8 5.4 %collective-permute-start.20 = (bf16[1024,512]{1,0:T(8,128)(2,1)S(1)}, bf16[1024,512]{1,0:T(8,128)(2,1)S(1)}, u32[]{:S(2)}, u32[]{:S(2)}) collective-permute-start(bf16[1024,512]{1,0:T(8,128)(2,1)S(1)} %convert_add_fusion), channel_id=1, source_target_pairs={{8,0},{12,4},{16,8},{20,12},{24,16},{28,20},{0,24},{4,28},{9,1},{1... | collective-permute-start | bytes 3145736 | tf_op jit(solution)/shard_map/ppermute | solution.py:263
  262.2 11.1 %collective-permute-done.14 = bf16[1024,512]{1,0:T(8,128)(2,1)S(1)} collective-permute-done((bf16[1024,512]{1,0:T(8,128)(2,1)S(1)}, bf16[1024,512]{1,0:T(8,128)(2,1)S(1)}, u32[]{:S(2)}, u32[]{:S(2)}) %collective-permute-start.14) | collective-permute-done | bytes 1048608 | tf_op jit(solution)/shard_map/ppermute | solution.py:256
  275.2 2.7 convolution_convert_fusion
  277.9 8.0 %collective-permute-done.20 = bf16[1024,512]{1,0:T(8,128)(2,1)S(1)} collective-permute-done((bf16[1024,512]{1,0:T(8,128)(2,1)S(1)}, bf16[1024,512]{1,0:T(8,128)(2,1)S(1)}, u32[]{:S(2)}, u32[]{:S(2)}) %collective-permute-start.20) | collective-permute-done | bytes 1048608 | tf_op jit(solution)/shard_map/ppermute | solution.py:263
  285.9 21.6 %collective-permute-done.19 = bf16[1024,512]{1,0:T(8,128)(2,1)S(1)} collective-permute-done((bf16[1024,512]{1,0:T(8,128)(2,1)S(1)}, bf16[1024,512]{1,0:T(8,128)(2,1)S(1)}, u32[]{:S(2)}, u32[]{:S(2)}) %collective-permute-start.19) | collective-permute-done | bytes 1048608 | tf_op jit(solution)/shard_map/ppermute | solution.py:263
  307.5 4.8 %multiply_convert_fusion = bf16[1024,512]{1,0:T(8,128)(2,1)} fusion(f32[512,512]{1,0:T(8,128)S(1)} %shard_map.42, bf16[1024,512]{1,0:T(8,128)(2,1)S(1)} %collective-permute-done.20, bf16[1024,512]{1,0:T(8,128)(2,1)S(1)} %collective-permute-done.19, bf16[1024,512]{1,0:T(8,128)(2,1)S(1)} %collective-permute-done.16, f32[2048,512]{1,0:T(8,128)S(1)} %fusion.10, ...), kind=kOutput, calls=%fused_computation.29 | convolution fusion | flops 3225419776 | bytes 7340036 | tf_op jit(solution)/shard_map/dot_general | solution.py:16
  (62 shorter events, 25.1 us)
Async XLA Ops:
  0.6 28.5 %collective-permute-start.1 = (bf16[1024,512]{1,0:T(8,128)(2,1)}, bf16[1024,512]{1,0:T(8,128)(2,1)S(1)}, u32[]{:S(2)}, u32[]{:S(2)}) collective-permute-start(bf16[1024,512]{1,0:T(8,128)(2,1)} %param.3), channel_id=1, source_target_pairs={{0,8},{4,12},{8,16},{12,20},{16,24},{20,28},{24,0},{28,4},{1,9},{5... | collective-permute-start | bytes 3145736 | tf_op jit(solution)/shard_map/ppermute | solution.py:188
  3.7 26.9 %collective-permute-start = (bf16[1024,512]{1,0:T(8,128)(2,1)}, bf16[1024,512]{1,0:T(8,128)(2,1)S(1)}, u32[]{:S(2)}, u32[]{:S(2)}) collective-permute-start(bf16[1024,512]{1,0:T(8,128)(2,1)} %param.3), channel_id=1, source_target_pairs={{0,4},{4,0},{8,12},{12,8},{16,20},{20,16},{24,28},{28,24},{1,5},{5... | collective-permute-start | bytes 3145736 | tf_op jit(solution)/shard_map/ppermute | solution.py:187
  29.1 27.9 %collective-permute-start.2 = (bf16[1024,512]{1,0:T(8,128)(2,1)S(1)}, bf16[1024,512]{1,0:T(8,128)(2,1)S(1)}, u32[]{:S(2)}, u32[]{:S(2)}) collective-permute-start(bf16[1024,512]{1,0:T(8,128)(2,1)S(1)} %collective-permute-done.1), channel_id=1, source_target_pairs={{0,4},{4,0},{8,12},{12,8},{16,20},{20,16},{24,28},{28,24},{1,5},{5... | collective-permute-start | bytes 3145736 | tf_op jit(solution)/shard_map/ppermute | solution.py:187
  30.6 25.6 %collective-permute-start.3 = (bf16[1024,512]{1,0:T(8,128)(2,1)S(1)}, bf16[1024,512]{1,0:T(8,128)(2,1)S(1)}, u32[]{:S(2)}, u32[]{:S(2)}) collective-permute-start(bf16[1024,512]{1,0:T(8,128)(2,1)S(1)} %collective-permute-done.1), channel_id=1, source_target_pairs={{0,8},{4,12},{8,16},{12,20},{16,24},{20,28},{24,0},{28,4},{1,9},{5... | collective-permute-start | bytes 3145736 | tf_op jit(solution)/shard_map/ppermute | solution.py:188
  56.2 26.5 %collective-permute-start.4 = (bf16[1024,512]{1,0:T(8,128)(2,1)S(1)}, bf16[1024,512]{1,0:T(8,128)(2,1)S(1)}, u32[]{:S(2)}, u32[]{:S(2)}) collective-permute-start(bf16[1024,512]{1,0:T(8,128)(2,1)S(1)} %collective-permute-done.3), channel_id=1, source_target_pairs={{0,4},{4,0},{8,12},{12,8},{16,20},{20,16},{24,28},{28,24},{1,5},{5... | collective-permute-start | bytes 3145736 | tf_op jit(solution)/shard_map/ppermute | solution.py:187
  57.0 24.7 %collective-permute-start.5 = (bf16[1024,512]{1,0:T(8,128)(2,1)S(1)}, bf16[1024,512]{1,0:T(8,128)(2,1)S(1)}, u32[]{:S(2)}, u32[]{:S(2)}) collective-permute-start(bf16[1024,512]{1,0:T(8,128)(2,1)S(1)} %collective-permute-done.3), channel_id=1, source_target_pairs={{0,8},{4,12},{8,16},{12,20},{16,24},{20,28},{24,0},{28,4},{1,9},{5... | collective-permute-start | bytes 3145736 | tf_op jit(solution)/shard_map/ppermute | solution.py:188
  81.7 13.5 %collective-permute-start.6 = (bf16[512,512]{1,0:T(8,128)(2,1)S(1)}, bf16[512,512]{1,0:T(8,128)(2,1)S(1)}, u32[]{:S(2)}, u32[]{:S(2)}) collective-permute-start(bf16[512,512]{1,0:T(8,128)(2,1)S(1)} %slice.36), channel_id=1, source_target_pairs={{0,4},{4,0},{8,12},{12,8},{16,20},{20,16},{24,28},{28,24},{1,5},{5... | collective-permute-start | bytes 1572872 | tf_op jit(solution)/shard_map/ppermute | solution.py:183
  82.8 12.4 %collective-permute-start.7 = (bf16[512,512]{1,0:T(8,128)(2,1)S(1)}, bf16[512,512]{1,0:T(8,128)(2,1)S(1)}, u32[]{:S(2)}, u32[]{:S(2)}) collective-permute-start(bf16[512,512]{1,0:T(8,128)(2,1)S(1)} %slice.37), channel_id=1, source_target_pairs={{0,8},{4,12},{8,16},{12,20},{16,24},{20,28},{24,0},{28,4},{1,9},{5... | collective-permute-start | bytes 1572872 | tf_op jit(solution)/shard_map/ppermute | solution.py:184
  100.9 2.0 copy-start
  103.0 4.4 %collective-permute-start.8 = (f32[2,512,512]{2,1,0:T(8,128)S(1)}, f32[2,512,512]{2,1,0:T(8,128)}, u32[]{:S(2)}, u32[]{:S(2)}) collective-permute-start(f32[2,512,512]{2,1,0:T(8,128)S(1)} %dynamic-slice_bitcast_fusion), channel_id=1, source_target_pairs={{0,1},{1,0},{2,3},{3,2},{4,5},{5,4},{6,7},{7,6},{8,9},{9,8},{10,11... | collective-permute-start | bytes 6291464 | tf_op jit(solution)/shard_map/ppermute | solution.py:211
  110.2 14.0 %collective-permute-start.9 = (bf16[512,512]{1,0:T(8,128)(2,1)S(1)}, bf16[512,512]{1,0:T(8,128)(2,1)S(1)}, u32[]{:S(2)}, u32[]{:S(2)}) collective-permute-start(bf16[512,512]{1,0:T(8,128)(2,1)S(1)} %fusion.42), channel_id=1, source_target_pairs={{0,2},{1,3},{2,0},{3,1},{4,6},{5,7},{6,4},{7,5},{8,10},{9,11},{10,... | collective-permute-start | bytes 1572872 | tf_op jit(solution)/shard_map/ppermute | solution.py:218
  124.4 13.3 %collective-permute-start.11 = (bf16[512,512]{1,0:T(8,128)(2,1)S(1)}, bf16[512,512]{1,0:T(8,128)(2,1)}, u32[]{:S(2)}, u32[]{:S(2)}) collective-permute-start(bf16[512,512]{1,0:T(8,128)(2,1)S(1)} %fusion.41), channel_id=1, source_target_pairs={{0,2},{1,3},{2,0},{3,1},{4,6},{5,7},{6,4},{7,5},{8,10},{9,11},{10,... | collective-permute-start | bytes 1572872 | tf_op jit(solution)/shard_map/ppermute | solution.py:224
  125.9 11.8 %collective-permute-start.10 = (bf16[512,512]{1,0:T(8,128)(2,1)S(1)}, bf16[512,512]{1,0:T(8,128)(2,1)}, u32[]{:S(2)}, u32[]{:S(2)}) collective-permute-start(bf16[512,512]{1,0:T(8,128)(2,1)S(1)} %fusion.41), channel_id=1, source_target_pairs={{0,1},{1,0},{2,3},{3,2},{4,5},{5,4},{6,7},{7,6},{8,9},{9,8},{10,11... | collective-permute-start | bytes 1572872 | tf_op jit(solution)/shard_map/ppermute | solution.py:223
  137.7 2.3 collective-permute-start.12
  141.3 1.3 copy-start.1
  145.9 23.8 %copy-start.2 = (bf16[2,2,512,512]{3,2,1,0:T(8,128)(2,1)S(1)}, bf16[2,2,512,512]{3,2,1,0:T(8,128)(2,1)}, u32[]{:S(2)}) copy-start(bf16[2,2,512,512]{3,2,1,0:T(8,128)(2,1)} %copy-done.1) | copy-start | bytes 6291460
  191.1 15.2 %collective-permute-start.17 = (bf16[512,512]{1,0:T(8,128)(2,1)S(1)}, bf16[512,512]{1,0:T(8,128)(2,1)S(1)}, u32[]{:S(2)}, u32[]{:S(2)}) collective-permute-start(bf16[512,512]{1,0:T(8,128)(2,1)S(1)} %get-tuple-element.24), channel_id=1, source_target_pairs={{0,4},{4,0},{8,12},{12,8},{16,20},{20,16},{24,28},{28,24},{1,5},{5... | collective-permute-start | bytes 1572872 | tf_op jit(solution)/shard_map/ppermute | solution.py:251
  193.6 35.1 %collective-permute-start.15 = (bf16[1024,512]{1,0:T(8,128)(2,1)S(1)}, bf16[1024,512]{1,0:T(8,128)(2,1)S(1)}, u32[]{:S(2)}, u32[]{:S(2)}) collective-permute-start(bf16[1024,512]{1,0:T(8,128)(2,1)S(1)} %dynamic-slice_convert_fusion.1), channel_id=1, source_target_pairs={{0,4},{4,0},{8,12},{12,8},{16,20},{20,16},{24,28},{28,24},{1,5},{5... | collective-permute-start | bytes 3145736 | tf_op jit(solution)/shard_map/ppermute | solution.py:256
  193.7 17.6 %collective-permute-start.13 = (bf16[512,512]{1,0:T(8,128)(2,1)S(1)}, bf16[512,512]{1,0:T(8,128)(2,1)S(1)}, u32[]{:S(2)}, u32[]{:S(2)}) collective-permute-start(bf16[512,512]{1,0:T(8,128)(2,1)S(1)} %get-tuple-element.25), channel_id=1, source_target_pairs={{0,8},{4,12},{8,16},{12,20},{16,24},{20,28},{24,0},{28,4},{1,9},{5... | collective-permute-start | bytes 1572872 | tf_op jit(solution)/shard_map/ppermute | solution.py:250
  202.2 75.7 %collective-permute-start.16 = (bf16[1024,512]{1,0:T(8,128)(2,1)S(1)}, bf16[1024,512]{1,0:T(8,128)(2,1)S(1)}, u32[]{:S(2)}, u32[]{:S(2)}) collective-permute-start(bf16[1024,512]{1,0:T(8,128)(2,1)S(1)} %dynamic-slice_convert_fusion), channel_id=1, source_target_pairs={{0,4},{4,0},{8,12},{12,8},{16,20},{20,16},{24,28},{28,24},{1,5},{5... | collective-permute-start | bytes 3145736 | tf_op jit(solution)/shard_map/ppermute | solution.py:256
  206.5 67.2 %collective-permute-start.18 = (bf16[1024,512]{1,0:T(8,128)(2,1)S(1)}, bf16[1024,512]{1,0:T(8,128)(2,1)S(1)}, u32[]{:S(2)}, u32[]{:S(2)}) collective-permute-start(bf16[1024,512]{1,0:T(8,128)(2,1)S(1)} %pad_maximum_fusion.2), channel_id=1, source_target_pairs={{0,8},{4,12},{8,16},{12,20},{16,24},{20,28},{24,0},{28,4},{1,9},{5... | collective-permute-start | bytes 3145736 | tf_op jit(solution)/shard_map/ppermute | solution.py:263
  211.5 61.8 %collective-permute-start.14 = (bf16[1024,512]{1,0:T(8,128)(2,1)S(1)}, bf16[1024,512]{1,0:T(8,128)(2,1)S(1)}, u32[]{:S(2)}, u32[]{:S(2)}) collective-permute-start(bf16[1024,512]{1,0:T(8,128)(2,1)S(1)} %pad_maximum_fusion.1), channel_id=1, source_target_pairs={{0,4},{4,0},{8,12},{12,8},{16,20},{20,16},{24,28},{28,24},{1,5},{5... | collective-permute-start | bytes 3145736 | tf_op jit(solution)/shard_map/ppermute | solution.py:256
  256.8 29.1 %collective-permute-start.20 = (bf16[1024,512]{1,0:T(8,128)(2,1)S(1)}, bf16[1024,512]{1,0:T(8,128)(2,1)S(1)}, u32[]{:S(2)}, u32[]{:S(2)}) collective-permute-start(bf16[1024,512]{1,0:T(8,128)(2,1)S(1)} %convert_add_fusion), channel_id=1, source_target_pairs={{8,0},{12,4},{16,8},{20,12},{24,16},{28,20},{0,24},{4,28},{9,1},{1... | collective-permute-start | bytes 3145736 | tf_op jit(solution)/shard_map/ppermute | solution.py:263
  274.1 33.4 %collective-permute-start.19 = (bf16[1024,512]{1,0:T(8,128)(2,1)S(1)}, bf16[1024,512]{1,0:T(8,128)(2,1)S(1)}, u32[]{:S(2)}, u32[]{:S(2)}) collective-permute-start(bf16[1024,512]{1,0:T(8,128)(2,1)S(1)} %add_convert_fusion), channel_id=1, source_target_pairs={{0,8},{4,12},{8,16},{12,20},{16,24},{20,28},{24,0},{28,4},{1,9},{5... | collective-permute-start | bytes 3145736 | tf_op jit(solution)/shard_map/ppermute | solution.py:263
